TPU v7x, 32 devices: a whole 2x2x4 slice. The times are simulated.
32 devices in a mesh: fsdp: 16 (over z, x, core), seq: 2 (over y).
Axes of the slice: x: 2, y: 2, z: 4, core: 2. Of those that a mesh axis runs over, the one named last changes fastest.
Arguments:
- tokens: bfloat16 [16, 1024, 1024], P('fsdp', 'seq'), may hold values from -6 to 6
- gain_a: bfloat16 [1024], P(('fsdp', 'seq')), may hold values from 0.5 to 1.5
- mix_in: bfloat16 [1024, 3072], P(('fsdp', 'seq')), may hold values from -0.1875 to 0.1875
- conv_tap: bfloat16 [3, 1024], P(None, ('fsdp', 'seq')), may hold values from -3.5 to 3.5
- mix_out: bfloat16 [1024, 1024], P(('fsdp', 'seq')), may hold values from -0.1875 to 0.1875
- gain_b: bfloat16 [1024], P(('fsdp', 'seq')), may hold values from 0.5 to 1.5
- ff_gate: bfloat16 [1024, 4608], P(('fsdp', 'seq')), may hold values from -0.1875 to 0.1875
- ff_up: bfloat16 [1024, 4608], P(('fsdp', 'seq')), may hold values from -0.1875 to 0.1875
- ff_down: bfloat16 [4608, 1024], P(('fsdp', 'seq')), may hold values from -0.125 to 0.125
- cotangent: bfloat16 [16, 1024, 1024], P('fsdp', 'seq'), may hold values from -6 to 6
Outputs:
- block_out: bfloat16 [16, 1024, 1024], P('fsdp', 'seq')
- grad_tokens: float32 [16, 1024, 1024], P('fsdp', 'seq')
- grad_gain_a: float32 [1024], P(('fsdp', 'seq'))
- grad_mix_in: float32 [1024, 3072], P(('fsdp', 'seq'))
- grad_conv_tap: float32 [3, 1024], P(None, ('fsdp', 'seq'))
- grad_mix_out: float32 [1024, 1024], P(('fsdp', 'seq'))
- grad_gain_b: float32 [1024], P(('fsdp', 'seq'))
- grad_ff_gate: float32 [1024, 4608], P(('fsdp', 'seq'))
- grad_ff_up: float32 [1024, 4608], P(('fsdp', 'seq'))
- grad_ff_down: float32 [4608, 1024], P(('fsdp', 'seq'))
All inputs are finite; a program needn't handle non-finite values.
Results may differ from a plain program's by a relative error of at most 0.0096.
Values may be sent and summed in bfloat16 or wider, within the bound.
No kernel may reach another device: no remote copies, remote signals or barrier semaphores. Data moves between devices by JAX's collectives and lax.ppermute only.
A program may use at most 256 MiB of HBM per device.

v0:
```python
import jax
import jax.numpy as jnp
from jax import lax
from jax.sharding import PartitionSpec as P

EPSILON = 1e-05


def shifted(shard, axis, by):
    size = lax.axis_size(axis)
    pairs = [(i, i + by) for i in range(size) if 0 <= i + by < size]
    return lax.ppermute(shard, axis, pairs)


def normalize(values, gain):
    scale = lax.rsqrt(jnp.mean(values * values, axis=-1, keepdims=True) + EPSILON)
    normalized_rows = values * scale
    return (normalized_rows, scale, normalized_rows * gain.astype(jnp.float32))


def norm_back(d_hidden, normalized_rows, scale, gain):
    norm_gradient = d_hidden * gain.astype(jnp.float32)
    grad_gain = jnp.sum(d_hidden * normalized_rows, axis=0)
    d_input = scale * (
        norm_gradient
        - normalized_rows * jnp.mean(norm_gradient * normalized_rows, axis=-1, keepdims=True)
    )
    return (d_input, grad_gain)


def dot_plain(left_segment, right_segment):
    return jnp.dot(left_segment, right_segment, preferred_element_type=jnp.float32)


def dot_first(left_segment, right_segment):
    return lax.dot_general(
        left_segment, right_segment, (((0,), (0,)), ((), ())), preferred_element_type=jnp.float32
    )


def dot_second(left_segment, right_segment):
    return lax.dot_general(
        left_segment, right_segment, (((1,), (1,)), ((), ())), preferred_element_type=jnp.float32
    )


def body(tokens, gain_a, mix_in, conv_tap, mix_out, gain_b, ff_gate, ff_up, ff_down, cotangent):
    seq_count, local_rows, feature_width = tokens.shape
    row_total = seq_count * local_rows
    tap_count = conv_tap.shape[0]
    gain_one, input_projection_weight, taps_whole, weight_out = (
        lax.all_gather(gain_a, ("fsdp", "seq"), axis=0, tiled=True),
        lax.all_gather(mix_in, ("fsdp", "seq"), axis=0, tiled=True),
        lax.all_gather(conv_tap, ("fsdp", "seq"), axis=1, tiled=True),
        lax.all_gather(mix_out, ("fsdp", "seq"), axis=0, tiled=True),
    )
    gain_two, weight_gate, weight_up, down_projection_weight = (
        lax.all_gather(gain_b, ("fsdp", "seq"), axis=0, tiled=True),
        lax.all_gather(ff_gate, ("fsdp", "seq"), axis=0, tiled=True),
        lax.all_gather(ff_up, ("fsdp", "seq"), axis=0, tiled=True),
        lax.all_gather(ff_down, ("fsdp", "seq"), axis=0, tiled=True),
    )
    inputs = tokens.reshape(row_total, feature_width).astype(jnp.float32)
    normed_a, scale_a, hidden = normalize(inputs, gain_one)
    hidden_low = hidden.astype(jnp.bfloat16)
    projected = dot_plain(hidden_low, input_projection_weight)
    b_part = projected[:, :feature_width]
    c_part = projected[:, feature_width : 2 * feature_width]
    v_part = projected[:, 2 * feature_width :]
    mixed = (b_part * v_part).astype(jnp.bfloat16).reshape(seq_count, local_rows, feature_width)
    edge_rows = shifted(mixed[:, local_rows - (tap_count - 1) :, :], "seq", 1)
    extended = jnp.concatenate([edge_rows, mixed], axis=1).astype(jnp.float32)
    tap_values = taps_whole.astype(jnp.float32)
    convolved = tap_values[0] * extended[:, 0:local_rows]
    for offset in range(1, tap_count):
        convolved = convolved + tap_values[offset] * extended[:, offset : offset + local_rows]
    convolved = convolved.reshape(row_total, feature_width)
    gated = (c_part * convolved).astype(jnp.bfloat16)
    after_mix = inputs + dot_plain(gated, weight_out)
    normed_b, scale_b, hidden_b = normalize(after_mix, gain_two)
    hidden_b_low = hidden_b.astype(jnp.bfloat16)
    gate_value = dot_plain(hidden_b_low, weight_gate)
    up_value = dot_plain(hidden_b_low, weight_up)
    sigmoid_gate = jax.nn.sigmoid(gate_value)
    silu_gate = gate_value * sigmoid_gate
    active = (silu_gate * up_value).astype(jnp.bfloat16)
    results = after_mix + dot_plain(active, down_projection_weight)
    block_out = results.astype(jnp.bfloat16).reshape(seq_count, local_rows, feature_width)
    gain_two, weight_gate, weight_up, down_projection_weight = (
        lax.all_gather(gain_b, ("fsdp", "seq"), axis=0, tiled=True),
        lax.all_gather(ff_gate, ("fsdp", "seq"), axis=0, tiled=True),
        lax.all_gather(ff_up, ("fsdp", "seq"), axis=0, tiled=True),
        lax.all_gather(ff_down, ("fsdp", "seq"), axis=0, tiled=True),
    )
    cot_low = cotangent.reshape(row_total, feature_width)
    cot_full = cot_low.astype(jnp.float32)
    d_active = dot_second(cot_low, down_projection_weight)
    d_up = (d_active * silu_gate).astype(jnp.bfloat16)
    d_gate = (
        d_active * up_value * sigmoid_gate * (1.0 + gate_value * (1.0 - sigmoid_gate))
    ).astype(jnp.bfloat16)
    gate_up_grads = jnp.concatenate([d_gate, d_up], axis=1)
    gate_up_owned = lax.psum_scatter(
        dot_first(hidden_b_low, gate_up_grads), ("fsdp", "seq"), scatter_dimension=0, tiled=True
    )
    down_owned = lax.psum_scatter(
        dot_first(active, cot_low), ("fsdp", "seq"), scatter_dimension=0, tiled=True
    )
    hidden_width = d_gate.shape[1]
    d_hidden_b = dot_second(d_gate, weight_gate) + dot_second(d_up, weight_up)
    d_norm_input, grad_gain_two = norm_back(d_hidden_b, normed_b, scale_b, gain_two)
    d_after = cot_full + d_norm_input
    gain_one, input_projection_weight, taps_whole, weight_out = (
        lax.all_gather(gain_a, ("fsdp", "seq"), axis=0, tiled=True),
        lax.all_gather(mix_in, ("fsdp", "seq"), axis=0, tiled=True),
        lax.all_gather(conv_tap, ("fsdp", "seq"), axis=1, tiled=True),
        lax.all_gather(mix_out, ("fsdp", "seq"), axis=0, tiled=True),
    )
    tap_values = taps_whole.astype(jnp.float32)
    d_branch = d_after.astype(jnp.bfloat16)
    d_gated = dot_second(d_branch, weight_out)
    d_c_part = d_gated * convolved
    d_conv = (d_gated * c_part).reshape(seq_count, local_rows, feature_width)
    grad_taps = jnp.stack(
        [
            jnp.sum(d_conv * extended[:, offset : offset + local_rows], axis=(0, 1))
            for offset in range(tap_count)
        ],
        axis=0,
    )
    padded_grad = jnp.pad(d_conv, ((0, 0), (tap_count - 1, tap_count - 1), (0, 0)))
    span = local_rows + tap_count - 1
    d_extended = tap_values[0] * padded_grad[:, tap_count - 1 : tap_count - 1 + span]
    for offset in range(1, tap_count):
        start_at = tap_count - 1 - offset
        d_extended = d_extended + tap_values[offset] * padded_grad[:, start_at : start_at + span]
    incoming = shifted(d_extended[:, : tap_count - 1, :], "seq", -1)
    incoming_full = jnp.pad(incoming, ((0, 0), (local_rows - (tap_count - 1), 0), (0, 0)))
    d_mixed = (d_extended[:, tap_count - 1 :, :] + incoming_full).reshape(row_total, feature_width)
    d_projected = jnp.concatenate([d_mixed * v_part, d_c_part, d_mixed * b_part], axis=-1).astype(
        jnp.bfloat16
    )
    grad_in_rows = dot_first(hidden_low, d_projected)
    grad_out_rows = dot_first(gated, d_branch)
    mixer_owned = lax.psum_scatter(
        jnp.concatenate([grad_in_rows, grad_out_rows], axis=1),
        ("fsdp", "seq"),
        scatter_dimension=0,
        tiled=True,
    )
    d_hidden = dot_second(d_projected, input_projection_weight)
    d_first_norm, grad_gain_one = norm_back(d_hidden, normed_a, scale_a, gain_one)
    grad_tokens = (d_after + d_first_norm).reshape(seq_count, local_rows, feature_width)
    small_terms = jnp.concatenate(
        [grad_gain_one[None, :], grad_gain_two[None, :], grad_taps], axis=0
    )
    small_owned = lax.psum_scatter(small_terms, ("fsdp", "seq"), scatter_dimension=1, tiled=True)
    return (
        block_out,
        grad_tokens,
        small_owned[0],
        mixer_owned[:, : 3 * feature_width],
        small_owned[2:],
        mixer_owned[:, 3 * feature_width :],
        small_owned[1],
        gate_up_owned[:, :hidden_width],
        gate_up_owned[:, hidden_width:],
        down_owned,
    )


def solution(mesh):
    return jax.shard_map(
        body,
        mesh=mesh,
        in_specs=(
            P("fsdp", "seq", None),
            P(("fsdp", "seq")),
            P(("fsdp", "seq"), None),
            P(None, ("fsdp", "seq")),
            P(("fsdp", "seq"), None),
            P(("fsdp", "seq")),
            P(("fsdp", "seq"), None),
            P(("fsdp", "seq"), None),
            P(("fsdp", "seq"), None),
            P("fsdp", "seq", None),
        ),
        out_specs=(
            P("fsdp", "seq", None),
            P("fsdp", "seq", None),
            P(("fsdp", "seq")),
            P(("fsdp", "seq"), None),
            P(None, ("fsdp", "seq")),
            P(("fsdp", "seq"), None),
            P(("fsdp", "seq")),
            P(("fsdp", "seq"), None),
            P(("fsdp", "seq"), None),
            P(("fsdp", "seq"), None),
        ),
        check_vma=False,
    )
```

profile of v0, /device:TPU:0, one launch (start us, length us, event | category | flops | bytes accessed | tf_op | source)
XLA Modules:
  0.0 1520.2 jit_solution(14274881013224123707)
XLA Ops:
  12.3 42.2 %all-reduce.4 = (bf16[1024]{0:T(1024)(128)(2,1)S(1)}, bf16[1024]{0:T(1024)(128)(2,1)S(1)}) all-reduce(bf16[1024]{0:T(1024)(128)(2,1)S(1)} %dynamic-update-slice, bf16[1024]{0:T(1024)(128)(2,1)S(1)} %dynamic-update-slice.1), channel_id=1, replica_groups=mesh['fsdp'=16,'seq'=2] {'fsdp','seq'}, use_global_device_ids=true, to_apply=%add.2 | all-reduce | flops 2048 | bytes 8192
  54.5 66.8 %all-gather = bf16[32,32,3]{1,2,0:T(4,128)(2,1)S(1)} all-gather(bf16[1,32,3]{1,2,0:T(4,128)(2,1)} %bitcast.94), channel_id=1, replica_groups=mesh['fsdp'=16,'seq'=2] {'fsdp','seq'}, dimensions={0}, use_global_device_ids=true | all-gather | bytes 6336 | tf_op jit(solution)/shard_map/all_gather | solution.py:54
  121.4 1.5 fusion.16
  122.9 5.7 fusion.33
  132.0 2.4 fusion.18
  134.4 7.3 all-gather.9.cloned.1.call-done
  141.7 3.3 multiply_reduce_fusion.5
  147.6 77.9 %all-gather.13.cloned.1.call-done = bf16[1024,4608]{1,0:T(8,128)(2,1)} async-done(((bf16[32,4608]{1,0:T(8,128)(2,1)}), bf16[1024,4608]{1,0:T(8,128)(2,1)}) %all-gather.13.cloned.1.call-update) | async-done | bytes 9437200 | tf_op jit(solution)/shard_map/all_gather | solution.py:60
  225.5 10.2 fusion.42
  235.7 73.2 %all-gather.11.cloned.1.call-done = bf16[1024,4608]{1,0:T(8,128)(2,1)} async-done(((bf16[32,4608]{1,0:T(8,128)(2,1)}), bf16[1024,4608]{1,0:T(8,128)(2,1)}) %all-gather.11.cloned.1.call-update) | async-done | bytes 9437200 | tf_op jit(solution)/shard_map/all_gather | solution.py:59
  309.0 10.1 fusion.41
  319.0 73.4 %all-gather.15.cloned.1.call-done = bf16[4608,1024]{1,0:T(8,128)(2,1)} async-done(((bf16[144,1024]{1,0:T(8,128)(2,1)}), bf16[4608,1024]{1,0:T(8,128)(2,1)}) %all-gather.15.cloned.1.call-update) | async-done | bytes 9437200 | tf_op jit(solution)/shard_map/all_gather | solution.py:61
  392.4 18.1 %multiply_convert_fusion = (bf16[512,4608]{1,0:T(8,128)(2,1)}, bf16[512,4608]{1,0:T(8,128)(2,1)}, bf16[512,4608]{1,0:T(8,128)(2,1)}) fusion(f32[512,4608]{1,0:T(8,128)} %fusion.41, f32[512,4608]{1,0:T(8,128)} %fusion.42, bf16[4608,1024]{1,0:T(8,128)(2,1)} %all-gather.15.cloned.1.call-done, bf16[1,512,1024]{2,1,0:T(8,128)(2,1)} %param.19), kind=kOutput, calls=%fused_computation.5 | convolution fusion | flops 4867227648 | bytes 43515904 | tf_op jit(solution)/shard_map/dot_general | solution.py:42
  410.5 9.2 fusion.43
  419.7 8.3 multiply_reduce_fusion.3
  429.3 3.4 fusion.28
  437.6 3.7 collective-permute-done.1
  442.2 6.9 fusion.21
  449.1 5.0 fusion.15
  455.2 11.8 pad_maximum_fusion
  468.2 21.3 %fusion = f32[1024,9216]{1,0:T(8,128)} fusion(bf16[512,1024]{1,0:T(8,128)(2,1)S(1)} %copy-done.10, bf16[512,4608]{1,0:T(8,128)(2,1)} %get-tuple-element.22, bf16[512,4608]{1,0:T(8,128)(2,1)} %get-tuple-element.23), kind=kOutput, calls=%fused_computation.1 | convolution fusion | flops 9682550784 | bytes 48234496 | tf_op jit(solution)/shard_map/dot_general | solution.py:36
  490.8 11.5 fusion.24
  502.3 1.6 copy-done.6
  503.9 9.9 fusion.20
  513.8 1.9 fusion.14
  515.7 71.8 %reduce-scatter.13.cloned.1.call-done = f32[32,5]{1,0:T(8,128)} async-done(((f32[1024,5]{1,0:T(8,128)}), f32[32,5]{1,0:T(8,128)}) %reduce-scatter.13.cloned.1.call-update) | async-done | bytes 656
  591.0 352.2 %reduce-scatter.7.cloned.1.call-done = f32[32,4096]{1,0:T(8,128)} async-done(((f32[1024,4096]{1,0:T(8,128)}), f32[32,4096]{1,0:T(8,128)}) %reduce-scatter.7.cloned.1.call-update) | async-done | bytes 524304 | tf_op jit(solution)/shard_map/reduce_scatter | solution.py:145
  943.2 1.6 slice.109
  944.8 1.8 slice.107
  946.6 353.8 %reduce-scatter.9.cloned.1.call-done = f32[32,9216]{1,0:T(8,128)} async-done(((f32[1024,9216]{1,0:T(8,128)}), f32[32,9216]{1,0:T(8,128)}) %reduce-scatter.9.cloned.1.call-update) | async-done | bytes 1179664 | tf_op jit(solution)/shard_map/reduce_scatter | solution.py:103
  1300.3 2.3 fusion.38
  1302.7 210.6 %reduce-scatter.11.cloned.1.call-done = f32[144,1024]{1,0:T(8,128)} async-done(((f32[4608,1024]{1,0:T(8,128)}), f32[144,1024]{1,0:T(8,128)}) %reduce-scatter.11.cloned.1.call-update) | async-done | bytes 589840 | tf_op jit(solution)/shard_map/reduce_scatter | solution.py:106
  (92 shorter events, 25.0 us)
Async XLA Ops:
  7.2 115.7 %copy-start.3 = (bf16[1,512,1024]{2,1,0:T(8,128)(2,1)S(1)}, bf16[1,512,1024]{2,1,0:T(8,128)(2,1)}, u32[]{:S(2)}) copy-start(bf16[1,512,1024]{2,1,0:T(8,128)(2,1)} %param.10) | copy-start | bytes 3145732
  7.2 115.7 %all-gather.7.cloned.1.call-start = ((), (), s32[]{:S(2)}) async-start(), calls=%async_computation.4 | async-start | bytes 6488064 | tf_op jit(solution)/shard_map/all_gather | solution.py:53
  7.9 133.7 %all-gather.9.cloned.1.call-start = ((), (), s32[]{:S(2)}) async-start(), calls=%async_computation.5 | async-start | bytes 2162688 | tf_op jit(solution)/shard_map/all_gather | solution.py:55
  8.7 216.9 %all-gather.13.cloned.1.call-start = ((), (), s32[]{:S(2)}) async-start(), calls=%async_computation.7 | async-start | bytes 9732096 | tf_op jit(solution)/shard_map/all_gather | solution.py:60
  9.4 299.6 %all-gather.11.cloned.1.call-start = ((), (), s32[]{:S(2)}) async-start(), calls=%async_computation.6 | async-start | bytes 9732096 | tf_op jit(solution)/shard_map/all_gather | solution.py:59
  10.0 382.4 %all-gather.15.cloned.1.call-start = ((), (), s32[]{:S(2)}) async-start(), calls=%async_computation.8 | async-start | bytes 9732096 | tf_op jit(solution)/shard_map/all_gather | solution.py:61
  10.6 577.0 %reduce-scatter.13.cloned.1.call-start = ((), (), s32[]{:S(2)}) async-start(), calls=%async_computation.12 | async-start | bytes 540672
  128.6 3.3 copy-start
  129.0 2.7 collective-permute-start
  144.9 1.3 copy-start.4
  410.5 9.2 copy-start.5
  410.5 9.2 copy-start.9
  419.7 8.3 copy-start.12
  428.1 1.2 copy-start.8
  428.1 6.2 slice-start
  429.3 3.4 copy-start.1
  429.3 3.7 copy-start.14
  429.3 5.0 slice-start.1
  435.1 2.0 copy-start.7
  435.8 5.5 collective-permute-start.1
  441.3 7.8 slice-start.2
  442.2 7.0 slice-start.3
  455.2 488.0 %reduce-scatter.7.cloned.1.call-start = ((), (), s32[]{:S(2)}) async-start(), calls=%async_computation.9 | async-start | bytes 17301504 | tf_op jit(solution)/shard_map/reduce_scatter | solution.py:145
  467.0 1.2 copy-start.10
  467.0 833.3 %reduce-scatter.9.cloned.1.call-start = ((), (), s32[]{:S(2)}) async-start(), calls=%async_computation.10 | async-start | bytes 38928384 | tf_op jit(solution)/shard_map/reduce_scatter | solution.py:103
  489.6 1.2 copy-start.13
  489.6 1023.7 %reduce-scatter.11.cloned.1.call-start = ((), (), s32[]{:S(2)}) async-start(), calls=%async_computation.11 | async-start | bytes 19464192 | tf_op jit(solution)/shard_map/reduce_scatter | solution.py:106
  502.3 1.6 copy-start.6
  503.9 9.9 copy-start.2
  503.9 9.9 copy-start.11
Sparse Core Ops, SparseCore 0:
  10.9 72.5 all-gather.6
  86.6 54.9 all-gather.8
  144.6 80.8 all-gather.12
  228.3 80.6 all-gather.10
  311.7 80.6 all-gather.14
  455.3 132.1 reduce-scatter.12
  589.9 353.2 reduce-scatter.6
  950.8 349.4 reduce-scatter.8
  1307.3 205.8 reduce-scatter.10
where the time goes:
time: 1530 us; the launch traced here: 1520 us
  waiting for transfers between devices  1230 us (80%)
  matrix products  124 us (8%)
  blocking collectives  109 us (7%)
  other arithmetic  22.9 us (1%)
  local copies, waits for them, and re-layouts  18.2 us (1%)
    reduce_scatter x1, waiting for transfers between devices, body(): lax.psum_scatter(dot_first(hidden_b_low, gate_up_grads), ('fsdp', 'seq'),...  354 us
    reduce_scatter x1, waiting for transfers between devices, body(): lax.psum_scatter(jnp.concatenate([grad_in_rows, grad_out_rows], axis=1),...  352 us
    reduce_scatter x1, waiting for transfers between devices, body(): lax.psum_scatter(dot_first(active, cot_low), ('fsdp', 'seq'), scatter_dim...  211 us
    all_gather x1, waiting for transfers between devices, body(): lax.all_gather(ff_up, ('fsdp', 'seq'), axis=0, tiled=True)  77.9 us
    unnamed x10, waiting for transfers between devices  75 us
    all_gather x1, waiting for transfers between devices, body(): lax.all_gather(ff_down, ('fsdp', 'seq'), axis=0, tiled=True)  73.4 us
    all_gather x1, waiting for transfers between devices, body(): lax.all_gather(ff_gate, ('fsdp', 'seq'), axis=0, tiled=True)  73.2 us
    all_gather x1, blocking collectives, body(): lax.all_gather(conv_tap, ('fsdp', 'seq'), axis=1, tiled=True)  66.8 us
  transfers between devices with their start and end apart: 11, of which 10 were waited for; matrix products, arithmetic and copies ran while one was open for 7% of the time, Pallas kernels for 0%

commit v1 on v0

v1 whole, which is shorter than its diff:
```python
import jax
import jax.numpy as jnp
from jax import lax
from jax.sharding import PartitionSpec as P

EPSILON = 1e-05
CORE = ("fsdp", 0)


def shifted(shard, axis, by):
    size = lax.axis_size(axis)
    pairs = [(i, i + by) for i in range(size) if 0 <= i + by < size]
    return lax.ppermute(shard, axis, pairs)


def bit_count(axis):
    return lax.axis_size(axis).bit_length() - 1


def my_bit(dim):
    axis, bit = dim
    return (lax.axis_index(axis) >> bit) & 1


def swap(value, dim):
    axis, bit = dim
    return lax.ppermute(value, axis, [(i, i ^ (1 << bit)) for i in range(lax.axis_size(axis))])


def rank(dim):
    axis, bit = dim
    return (0 if axis == "fsdp" else 1, -bit)


def routes():
    near = [("fsdp", b) for b in range(1, min(2, bit_count("fsdp")))]
    far = [("fsdp", b) for b in range(2, bit_count("fsdp"))]
    along = [("seq", b) for b in range(bit_count("seq"))]
    return (far + near + along, far[::-1] + along + near)


def gather_step(buffer, held, dim):
    other = swap(buffer, dim)
    axis = sum(rank(h) < rank(dim) for h in held)
    high = my_bit(dim) == 1
    merged = jnp.stack(
        [jnp.where(high, other, buffer), jnp.where(high, buffer, other)], axis=axis
    )
    return merged, held + [dim]


def gather(piece, held, order):
    held = list(held)
    for dim in order:
        piece, held = gather_step(piece, held, dim)
    return piece


def scatter_step(buffer, held, dim, last):
    axis = sum(rank(h) < rank(dim) for h in held)
    bit = my_bit(dim)
    keep = lax.dynamic_index_in_dim(buffer, bit, axis, keepdims=False)
    send = lax.dynamic_index_in_dim(buffer, 1 - bit, axis, keepdims=False)
    total = keep.astype(jnp.float32) + swap(send, dim).astype(jnp.float32)
    return (total if last else total.astype(jnp.bfloat16)), [h for h in held if h != dim]


def scatter(buffer, held, order):
    held = list(held)
    for step, dim in enumerate(order):
        buffer, held = scatter_step(buffer, held, dim, step == len(order) - 1)
    return buffer


def normalize(values, gain):
    scale = lax.rsqrt(jnp.mean(values * values, axis=-1, keepdims=True) + EPSILON)
    normalized_rows = values * scale
    return (normalized_rows, scale, normalized_rows * gain)


def norm_back(d_hidden, normalized_rows, scale, gain):
    norm_gradient = d_hidden * gain
    grad_gain = jnp.sum(d_hidden * normalized_rows, axis=0)
    d_input = scale * (
        norm_gradient
        - normalized_rows * jnp.mean(norm_gradient * normalized_rows, axis=-1, keepdims=True)
    )
    return (d_input, grad_gain)


def dot_plain(left_segment, right_segment):
    return jnp.dot(left_segment, right_segment, preferred_element_type=jnp.float32)


def dot_first(left_segment, right_segment):
    return lax.dot_general(
        left_segment, right_segment, (((0,), (0,)), ((), ())), preferred_element_type=jnp.float32
    )


def dot_second(left_segment, right_segment):
    return lax.dot_general(
        left_segment, right_segment, (((1,), (1,)), ((), ())), preferred_element_type=jnp.float32
    )


def core_columns(shard, core):
    rows, width = shard.shape
    high = lax.axis_size("fsdp") // 2
    return lax.dynamic_index_in_dim(
        shard.reshape(rows, high, 2, width // (2 * high)), core, 2, keepdims=False
    ).reshape(rows, width // 2)


def body(tokens, gain_a, mix_in, conv_tap, mix_out, gain_b, ff_gate, ff_up, ff_down, cotangent):
    seq_count, local_rows, feature_width = tokens.shape
    row_total = seq_count * local_rows
    tap_count = conv_tap.shape[0]
    own_rows = mix_in.shape[0]
    core = my_bit(CORE)
    route_a, route_b = routes()
    full = 2 * (1 << len(route_a))

    small = jnp.concatenate([gain_a[None], gain_b[None], conv_tap], axis=0).T
    small = jnp.pad(small, ((0, 0), (0, 128 - small.shape[1])))
    half_width = 2 * feature_width
    mixer_a = gather(mix_in[:, :half_width], [], route_a + [CORE])
    mixer_b = gather(
        jnp.concatenate([mix_in[:, half_width:], mix_out, small], axis=1), [], route_b + [CORE]
    )
    weight_bc = mixer_a.reshape(feature_width, half_width)
    mixer_b = mixer_b.reshape(feature_width, half_width + 128)
    weight_v = mixer_b[:, :feature_width]
    weight_out = mixer_b[:, feature_width:half_width]
    small_whole = mixer_b[:, half_width : half_width + 2 + tap_count].T.astype(jnp.float32)
    gain_one, gain_two, tap_values = small_whole[0], small_whole[1], small_whole[2:]

    def gate_like(shard, order):
        mine = core_columns(shard, core)
        piece, held = mine, []
        other = swap(core_columns(shard, 1 - core), CORE)
        high = core == 1
        piece = jnp.stack([jnp.where(high, other, mine), jnp.where(high, mine, other)], axis=0)
        return gather(piece, [CORE], order).reshape(feature_width, -1)

    weight_gate = gate_like(ff_gate, route_a)
    weight_up = gate_like(ff_up, route_b)
    down_half = feature_width // 2
    weight_down_a = gather(ff_down[:, :down_half], [], route_a).reshape(-1, down_half)
    weight_down_b = gather(ff_down[:, down_half:], [], route_b).reshape(-1, down_half)
    weight_down = jnp.concatenate([weight_down_a, weight_down_b], axis=1)

    cot_low = cotangent.reshape(row_total, feature_width)
    cot_full = cot_low.astype(jnp.float32)
    cot_pair = jnp.concatenate([cot_low, swap(cot_low, CORE)], axis=0)

    inputs = tokens.reshape(row_total, feature_width).astype(jnp.float32)
    normed_a, scale_a, hidden = normalize(inputs, gain_one)
    hidden_low = hidden.astype(jnp.bfloat16)
    bc_part = dot_plain(hidden_low, weight_bc)
    b_part = bc_part[:, :feature_width]
    c_part = bc_part[:, feature_width:]
    v_part = dot_plain(hidden_low, weight_v)
    mixed = (b_part * v_part).astype(jnp.bfloat16).reshape(seq_count, local_rows, feature_width)
    edge_rows = shifted(mixed[:, local_rows - (tap_count - 1) :, :], "seq", 1)
    extended = jnp.concatenate([edge_rows, mixed], axis=1).astype(jnp.float32)
    convolved = tap_values[0] * extended[:, 0:local_rows]
    for offset in range(1, tap_count):
        convolved = convolved + tap_values[offset] * extended[:, offset : offset + local_rows]
    convolved = convolved.reshape(row_total, feature_width)
    gated = (c_part * convolved).astype(jnp.bfloat16)
    after_mix = inputs + dot_plain(gated, weight_out)
    normed_b, scale_b, hidden_b = normalize(after_mix, gain_two)
    hidden_b_low = hidden_b.astype(jnp.bfloat16)
    hidden_pair = jnp.concatenate([hidden_b_low, swap(hidden_b_low, CORE)], axis=0)

    gate_value = dot_plain(hidden_pair, weight_gate)
    up_value = dot_plain(hidden_pair, weight_up)
    sigmoid_gate = jax.nn.sigmoid(gate_value)
    silu_gate = gate_value * sigmoid_gate
    active = (silu_gate * up_value).astype(jnp.bfloat16)

    held = [d for d in route_a]
    held_core = held + [CORE]
    shape = (2,) * len(held)
    grad_down = dot_first(active, cot_pair).astype(jnp.bfloat16)
    grad_down = grad_down.reshape(shape + (-1, feature_width))
    down_owned = jnp.concatenate(
        [
            scatter(grad_down[..., :down_half], held, route_a[::-1]),
            scatter(grad_down[..., down_half:], held, route_b[::-1]),
        ],
        axis=-1,
    )

    d_active = dot_second(cot_pair, weight_down)
    d_up = (d_active * silu_gate).astype(jnp.bfloat16)
    d_gate = (
        d_active * up_value * sigmoid_gate * (1.0 + gate_value * (1.0 - sigmoid_gate))
    ).astype(jnp.bfloat16)

    def owned_gate_like(gradient, order):
        gradient = gradient.astype(jnp.bfloat16).reshape(shape + (2, own_rows, -1))
        owned = scatter(gradient, held_core, order)
        mine = lax.dynamic_index_in_dim(owned, core, 0, keepdims=False)
        other = swap(lax.dynamic_index_in_dim(owned, 1 - core, 0, keepdims=False), CORE)
        high = lax.axis_size("fsdp") // 2
        mine, other = (v.reshape(own_rows, high, -1) for v in (mine, other))
        both = jnp.stack(
            [jnp.where(core == 1, other, mine), jnp.where(core == 1, mine, other)], axis=2
        )
        return both.reshape(own_rows, -1)

    up_owned = owned_gate_like(dot_first(hidden_pair, d_up), route_b[::-1])
    gate_owned = owned_gate_like(dot_first(hidden_pair, d_gate), route_a[::-1])

    d_hidden_pair = dot_second(d_gate, weight_gate) + dot_second(d_up, weight_up)
    d_hidden_b = d_hidden_pair[:row_total] + swap(d_hidden_pair[row_total:], CORE)
    d_norm_input, grad_gain_two = norm_back(d_hidden_b, normed_b, scale_b, gain_two)
    d_after = cot_full + d_norm_input

    out_pair = dot_plain(active, weight_down)
    results = after_mix + out_pair[:row_total] + swap(out_pair[row_total:], CORE)
    block_out = results.astype(jnp.bfloat16).reshape(seq_count, local_rows, feature_width)

    d_branch = d_after.astype(jnp.bfloat16)
    d_gated = dot_second(d_branch, weight_out)
    d_c_part = d_gated * convolved
    d_conv = (d_gated * c_part).reshape(seq_count, local_rows, feature_width)
    grad_taps = jnp.stack(
        [
            jnp.sum(d_conv * extended[:, offset : offset + local_rows], axis=(0, 1))
            for offset in range(tap_count)
        ],
        axis=0,
    )
    padded_grad = jnp.pad(d_conv, ((0, 0), (tap_count - 1, tap_count - 1), (0, 0)))
    span = local_rows + tap_count - 1
    d_extended = tap_values[0] * padded_grad[:, tap_count - 1 : tap_count - 1 + span]
    for offset in range(1, tap_count):
        start_at = tap_count - 1 - offset
        d_extended = d_extended + tap_values[offset] * padded_grad[:, start_at : start_at + span]
    incoming = shifted(d_extended[:, : tap_count - 1, :], "seq", -1)
    incoming_full = jnp.pad(incoming, ((0, 0), (local_rows - (tap_count - 1), 0), (0, 0)))
    d_mixed = (d_extended[:, tap_count - 1 :, :] + incoming_full).reshape(row_total, feature_width)
    d_b = (d_mixed * v_part).astype(jnp.bfloat16)
    d_c = d_c_part.astype(jnp.bfloat16)
    d_v = (d_mixed * b_part).astype(jnp.bfloat16)
    d_bc = jnp.concatenate([d_b, d_c], axis=1)
    grad_a = dot_first(hidden_low, d_bc).astype(jnp.bfloat16)
    grad_b = jnp.concatenate(
        [
            dot_first(gated, d_branch).astype(jnp.bfloat16),
            dot_first(hidden_low, d_v).astype(jnp.bfloat16),
        ],
        axis=1,
    )
    shape_all = (2,) * len(held_core) + (own_rows, half_width)
    owned_a = scatter(grad_a.reshape(shape_all), held_core, [CORE] + route_a[::-1])
    owned_b = scatter(grad_b.reshape(shape_all), held_core, [CORE] + route_b[::-1])

    d_hidden = dot_second(d_bc, weight_bc) + dot_second(d_v, weight_v)
    d_first_norm, grad_gain_one = norm_back(d_hidden, normed_a, scale_a, gain_one)
    grad_tokens = (d_after + d_first_norm).reshape(seq_count, local_rows, feature_width)
    small_terms = jnp.concatenate(
        [grad_gain_one[None, :], grad_gain_two[None, :], grad_taps], axis=0
    )
    for dim in [CORE] + route_a:
        small_terms = small_terms + swap(small_terms, dim)
    place = lax.axis_index("fsdp") * lax.axis_size("seq") + lax.axis_index("seq")
    small_owned = lax.dynamic_slice_in_dim(small_terms, place * own_rows, own_rows, axis=1)
    return (
        block_out,
        grad_tokens,
        small_owned[0],
        jnp.concatenate([owned_a, owned_b[:, feature_width:]], axis=1),
        small_owned[2:],
        owned_b[:, :feature_width],
        small_owned[1],
        gate_owned,
        up_owned,
        down_owned,
    )


def solution(mesh):
    return jax.shard_map(
        body,
        mesh=mesh,
        in_specs=(
            P("fsdp", "seq", None),
            P(("fsdp", "seq")),
            P(("fsdp", "seq"), None),
            P(None, ("fsdp", "seq")),
            P(("fsdp", "seq"), None),
            P(("fsdp", "seq")),
            P(("fsdp", "seq"), None),
            P(("fsdp", "seq"), None),
            P(("fsdp", "seq"), None),
            P("fsdp", "seq", None),
        ),
        out_specs=(
            P("fsdp", "seq", None),
            P("fsdp", "seq", None),
            P(("fsdp", "seq")),
            P(("fsdp", "seq"), None),
            P(None, ("fsdp", "seq")),
            P(("fsdp", "seq"), None),
            P(("fsdp", "seq")),
            P(("fsdp", "seq"), None),
            P(("fsdp", "seq"), None),
            P(("fsdp", "seq"), None),
        ),
        check_vma=False,
    )
```

time: 1530 us -> 608 us (0.40)
  waiting for transfers between devices: 1230 us -> 329 us
  blocking collectives: 109 us -> 0 us
  starting transfers between devices: 3.01 us -> 59.2 us
  local copies, waits for them, and re-layouts: 18.2 us -> 51.4 us
  other arithmetic: 22.9 us -> 51.9 us
  matrix products: 124 us -> 104 us
    reduce_scatter x3 -> x0, waiting for transfers between devices: 917 us -> none  [the longest x1 354 us: body(): lax.psum_scatter(dot_first(hidden_b_low, gate_up_grads), ('fsdp', 'seq'),...]
    ppermute x0 -> x65, waiting for transfers between devices: none -> 289 us  [swap(): lax.ppermute(value, axis, [(i, i ^ 1 << bit) for i in range(lax.axis_size...]
    all_gather x5 -> x0, waiting for transfers between devices: 232 us -> none  [the longest x1 77.9 us: body(): lax.all_gather(ff_up, ('fsdp', 'seq'), axis=0, tiled=True)]
    unnamed x10 -> x0, waiting for transfers between devices: 75 us -> none
    all_gather x1 -> x0, blocking collectives: 66.8 us -> none  [body(): lax.all_gather(conv_tap, ('fsdp', 'seq'), axis=1, tiled=True)]
    ppermute x0 -> x65, starting transfers between devices: none -> 54.9 us  [swap(): lax.ppermute(value, axis, [(i, i ^ 1 << bit) for i in range(lax.axis_size...]
    unnamed x1 -> x0, blocking collectives: 42.2 us -> none
    ppermute x2, waiting for transfers between devices: 5.01 us -> 40.7 us  [shifted(): return lax.ppermute(shard, axis, pairs)]
  transfers between devices with their start and end apart: 11 -> 67, of which waited for: 10 -> 33; matrix products, arithmetic and copies ran while one was open for 7% -> 26% of each run, Pallas kernels for 0% -> 0%
where the time goes in v1:
time: 608 us; the launch traced here: 599 us
  waiting for transfers between devices  329 us (54%)
  matrix products  104 us (17%)
  starting transfers between devices  59.2 us (10%)
  other arithmetic  51.9 us (9%)
  local copies, waits for them, and re-layouts  51.4 us (8%)
    ppermute x65, waiting for transfers between devices, swap(): lax.ppermute(value, axis, [(i, i ^ 1 << bit) for i in range(lax.axis_size...  289 us
    ppermute x65, starting transfers between devices, swap(): lax.ppermute(value, axis, [(i, i ^ 1 << bit) for i in range(lax.axis_size...  54.9 us
    ppermute x2, waiting for transfers between devices, shifted(): return lax.ppermute(shard, axis, pairs)  40.7 us
    dot_general x6, matrix products, dot_plain(): jnp.dot(left_segment, right_segment, preferred_element_type=jnp.float32)  40 us
    dot_general x6, matrix products, dot_second(): lax.dot_general(left_segment, right_segment, (((1,), (1,)), ((), ())), pr...  32.8 us
    dot_general x6, matrix products, dot_first(): lax.dot_general(left_segment, right_segment, (((0,), (0,)), ((), ())), pr...  31.6 us
    another operation x51, other arithmetic, gather_step(): jnp.stack([jnp.where(high, other, buffer), jnp.where(high, buffer, other)...  16 us
    convert_element_type x20, other arithmetic, scatter_step(): total.astype(jnp.bfloat16)  12.5 us
  transfers between devices with their start and end apart: 67, of which 33 were waited for; matrix products, arithmetic and copies ran while one was open for 26% of the time, Pallas kernels for 0%

profile of v1, /device:TPU:0, one launch (start us, length us, event | category | flops | bytes accessed | tf_op | source)
XLA Modules:
  0.0 598.9 jit_solution(12858987075984197707)
XLA Ops:
  17.3 4.3 collective-permute-done.5
  31.4 10.4 %collective-permute-done.6 = bf16[2,32,2048]{2,1,0:T(8,128)(2,1)S(1)} collective-permute-done((bf16[2,32,2048]{2,1,0:T(8,128)(2,1)S(1)}, bf16[2,32,2048]{2,1,0:T(8,128)(2,1)S(1)}, u32[]{:S(2)}, u32[]{:S(2)}) %collective-permute-start.6) | collective-permute-done | bytes 262176 | tf_op jit(solution)/shard_map/ppermute | solution.py:27
  41.9 7.7 %collective-permute-done.1 = bf16[2,32,2176]{2,1,0:T(8,128)(2,1)S(1)} collective-permute-done((bf16[2,32,2176]{2,1,0:T(8,128)(2,1)S(1)}, bf16[2,32,2176]{2,1,0:T(8,128)(2,1)S(1)}, u32[]{:S(2)}, u32[]{:S(2)}) %collective-permute-start.1) | collective-permute-done | bytes 278560 | tf_op jit(solution)/shard_map/ppermute | solution.py:27
  49.8 6.3 %collective-permute-done.13 = bf16[2,32,2304]{2,1,0:T(8,128)(2,1)S(1)} collective-permute-done((bf16[2,32,2304]{2,1,0:T(8,128)(2,1)S(1)}, bf16[2,32,2304]{2,1,0:T(8,128)(2,1)S(1)}, u32[]{:S(2)}, u32[]{:S(2)}) %collective-permute-start.13) | collective-permute-done | bytes 294944 | tf_op jit(solution)/shard_map/ppermute | solution.py:27
  59.4 7.3 %collective-permute-done.23 = bf16[2,144,512]{2,1,0:T(8,128)(2,1)S(1)} collective-permute-done((bf16[2,144,512]{2,1,0:T(8,128)(2,1)S(1)}, bf16[2,144,512]{2,1,0:T(8,128)(2,1)S(1)}, u32[]{:S(2)}, u32[]{:S(2)}) %collective-permute-start.23) | collective-permute-done | bytes 294944 | tf_op jit(solution)/shard_map/ppermute | solution.py:27
  73.8 21.5 %collective-permute-done.14 = bf16[2,2,32,2304]{3,2,1,0:T(8,128)(2,1)S(1)} collective-permute-done((bf16[2,2,32,2304]{3,2,1,0:T(8,128)(2,1)S(1)}, bf16[2,2,32,2304]{3,2,1,0:T(8,128)(2,1)S(1)}, u32[]{:S(2)}, u32[]{:S(2)}) %collective-permute-start.14) | collective-permute-done | bytes 589856 | tf_op jit(solution)/shard_map/ppermute | solution.py:27
  100.4 21.0 %collective-permute-done.8 = bf16[2,2,2,32,2048]{4,3,2,1,0:T(8,128)(2,1)S(1)} collective-permute-done((bf16[2,2,2,32,2048]{4,3,2,1,0:T(8,128)(2,1)S(1)}, bf16[2,2,2,32,2048]{4,3,2,1,0:T(8,128)(2,1)S(1)}, u32[]{:S(2)}, u32[]{:S(2)}) %collective-permute-start.8) | collective-permute-done | bytes 1048608 | tf_op jit(solution)/shard_map/ppermute | solution.py:27
  126.5 23.3 %collective-permute-done.15 = bf16[2,2,2,32,2304]{4,3,2,1,0:T(8,128)(2,1)S(1)} collective-permute-done((bf16[2,2,2,32,2304]{4,3,2,1,0:T(8,128)(2,1)S(1)}, bf16[2,2,2,32,2304]{4,3,2,1,0:T(8,128)(2,1)S(1)}, u32[]{:S(2)}, u32[]{:S(2)}) %collective-permute-start.15) | collective-permute-done | bytes 1179680 | tf_op jit(solution)/shard_map/ppermute | solution.py:27
  152.4 18.4 %collective-permute-done.25 = bf16[2,2,2,144,512]{4,3,2,1,0:T(8,128)(2,1)S(1)} collective-permute-done((bf16[2,2,2,144,512]{4,3,2,1,0:T(8,128)(2,1)S(1)}, bf16[2,2,2,144,512]{4,3,2,1,0:T(8,128)(2,1)S(1)}, u32[]{:S(2)}, u32[]{:S(2)}) %collective-permute-start.25) | collective-permute-done | bytes 1179680 | tf_op jit(solution)/shard_map/ppermute | solution.py:27
  186.5 8.9 %fusion.5 = f32[1024,2304]{1,0:T(8,128)} fusion(bf16[2304,512]{1,0:T(8,128)(2,1)S(1)} %bitcast.419, bf16[2304,512]{1,0:T(8,128)(2,1)S(1)} %bitcast.417, bf16[512,1024]{1,0:T(8,128)(2,1)} %collective-permute-done.31, bf16[512,1024]{1,0:T(8,128)(2,1)} %bitcast.83), kind=kOutput, calls=%fused_computation.23 | convolution fusion | flops 4845469696 | bytes 16252928 | tf_op jit(solution)/shard_map/dot_general | solution.py:102
  195.3 26.9 %collective-permute-done.10 = bf16[1,2,1024]{2,1,0:T(2,128)(2,1)S(1)} collective-permute-done((bf16[1,2,1024]{2,1,0:T(2,128)(2,1)S(1)}, bf16[1,2,1024]{2,1,0:T(2,128)(2,1)S(1)}, u32[]{:S(2)}, u32[]{:S(2)}) %collective-permute-start.10) | collective-permute-done | bytes 4128 | tf_op jit(solution)/shard_map/ppermute | solution.py:13
  234.5 8.2 %fusion.72 = f32[1024,2304]{1,0:T(8,128)} fusion(bf16[1024,2304]{1,0:T(8,128)(2,1)S(1)} %bitcast.409, bf16[512,1024]{1,0:T(8,128)(2,1)S(1)} %collective-permute-done.11, bf16[512,1024]{1,0:T(8,128)(2,1)S(1)} %multiply_convert_fusion.5), kind=kOutput, calls=%fused_computation.285 | convolution fusion | flops 4836032512 | bytes 16252928 | tf_op jit(solution)/shard_map/dot_general | solution.py:92
  242.7 17.2 %multiply_convert_fusion.1 = (bf16[1024,2304]{1,0:T(8,128)(2,1)}, bf16[1024,2304]{1,0:T(8,128)(2,1)}, bf16[1024,2304]{1,0:T(8,128)(2,1)}) fusion(f32[1024,2304]{1,0:T(8,128)} %fusion.5, f32[1024,2304]{1,0:T(8,128)} %fusion.72, bf16[1024,2304]{1,0:T(8,128)(2,1)} %bitcast.405, bf16[512,1024]{1,0:T(8,128)(2,1)} %copy-done.47, ...), kind=kOutput, calls=%fused_computation.1 | convolution fusion | flops 4871421952 | bytes 39845888 | tf_op jit(solution)/shard_map/dot_general | solution.py:92
  260.0 9.5 %fusion.6 = f32[1024,1024]{1,0:T(8,128)} fusion(bf16[1024,2304]{1,0:T(8,128)(2,1)} %get-tuple-element.31, bf16[2304,512]{1,0:T(8,128)(2,1)} %bitcast.420, bf16[2304,512]{1,0:T(8,128)(2,1)S(1)} %bitcast.418), kind=kOutput, calls=%fused_computation.24 | convolution fusion | flops 4841275392 | bytes 13631488 | tf_op jit(solution)/shard_map/dot_general | solution.py:92
  269.5 6.9 %convolution_convert_fusion = bf16[2304,1024]{1,0:T(8,128)(2,1)S(1)} fusion(bf16[1024,2304]{1,0:T(8,128)(2,1)S(1)} %copy-done.50, bf16[512,1024]{1,0:T(8,128)(2,1)} %collective-permute-done.31, bf16[512,1024]{1,0:T(8,128)(2,1)} %bitcast.83), kind=kOutput, calls=%fused_computation.5 | convolution fusion | flops 4838391808 | bytes 11534336 | tf_op jit(solution)/shard_map/dot_general | solution.py:96
  283.8 9.1 %fusion.80 = f32[1024,1024]{1,0:T(8,128)} fusion(bf16[1024,2304]{1,0:T(8,128)(2,1)} %get-tuple-element.30, bf16[1024,2304]{1,0:T(8,128)(2,1)S(1)} %bitcast.412), kind=kOutput, calls=%fused_computation.290 | convolution fusion | flops 4831838208 | bytes 13631488 | tf_op jit(solution)/shard_map/dot_general | solution.py:102
  292.9 7.9 %convolution_convert_fusion.1 = bf16[1024,2304]{1,0:T(8,128)(2,1)S(1)} fusion(bf16[1024,2304]{1,0:T(8,128)(2,1)} %get-tuple-element.30, bf16[512,1024]{1,0:T(8,128)(2,1)S(1)} %copy-done.48, bf16[512,1024]{1,0:T(8,128)(2,1)S(1)} %multiply_convert_fusion.5), kind=kOutput, calls=%fused_computation.6 | convolution fusion | flops 4838391808 | bytes 11534336 | tf_op jit(solution)/shard_map/dot_general | solution.py:96
  305.8 8.3 %convolution_add_fusion = f32[1024,1024]{1,0:T(8,128)S(1)} fusion(f32[1024,1024]{1,0:T(8,128)} %fusion.80, bf16[1024,2304]{1,0:T(8,128)(2,1)} %get-tuple-element.29, bf16[1024,2304]{1,0:T(8,128)(2,1)S(1)} %bitcast.408), kind=kOutput, calls=%fused_computation.102 | convolution fusion | flops 4832886784 | bytes 17825792 | tf_op jit(solution)/shard_map/dot_general | solution.py:102
  315.6 8.1 %convolution_convert_fusion.2 = bf16[1024,2304]{1,0:T(8,128)(2,1)S(1)} fusion(bf16[1024,2304]{1,0:T(8,128)(2,1)} %get-tuple-element.29, bf16[512,1024]{1,0:T(8,128)(2,1)S(1)} %copy-done.49, bf16[512,1024]{1,0:T(8,128)(2,1)S(1)} %copy-done.29), kind=kOutput, calls=%fused_computation.7 | convolution fusion | flops 4838391808 | bytes 11534336 | tf_op jit(solution)/shard_map/dot_general | solution.py:96
  327.7 45.9 %collective-permute-done.60 = bf16[2,2,144,512]{3,2,1,0:T(8,128)(2,1)S(1)} collective-permute-done((bf16[2,2,144,512]{3,2,1,0:T(8,128)(2,1)S(1)}, bf16[2,2,144,512]{3,2,1,0:T(8,128)(2,1)S(1)}, u32[]{:S(2)}, u32[]{:S(2)}) %collective-permute-start.60) | collective-permute-done | bytes 589856 | tf_op jit(solution)/shard_map/ppermute | solution.py:27
  374.3 13.8 %collective-permute-done.61 = bf16[2,144,512]{2,1,0:T(8,128)(2,1)S(1)} collective-permute-done((bf16[2,144,512]{2,1,0:T(8,128)(2,1)S(1)}, bf16[2,144,512]{2,1,0:T(8,128)(2,1)S(1)}, u32[]{:S(2)}, u32[]{:S(2)}) %collective-permute-start.61) | collective-permute-done | bytes 294944 | tf_op jit(solution)/shard_map/ppermute | solution.py:27
  388.9 8.2 %collective-permute-done.65 = bf16[2,144,512]{2,1,0:T(8,128)(2,1)S(1)} collective-permute-done((bf16[2,144,512]{2,1,0:T(8,128)(2,1)S(1)}, bf16[2,144,512]{2,1,0:T(8,128)(2,1)S(1)}, u32[]{:S(2)}, u32[]{:S(2)}) %collective-permute-start.65) | collective-permute-done | bytes 294944 | tf_op jit(solution)/shard_map/ppermute | solution.py:27
  412.4 13.7 %collective-permute-done.33 = f32[1,2,1024]{2,1,0:T(2,128)S(1)} collective-permute-done((f32[1,2,1024]{2,1,0:T(2,128)S(1)}, f32[1,2,1024]{2,1,0:T(2,128)S(1)}, u32[]{:S(2)}, u32[]{:S(2)}) %collective-permute-start.33) | collective-permute-done | bytes 8224 | tf_op jit(solution)/shard_map/ppermute | solution.py:13
  428.6 4.5 convolution_convert_fusion.3
  453.5 6.7 %copy.76 = bf16[1024,2048]{1,0:T(8,128)(2,1)} copy(bf16[1024,2048]{0,1:T(8,128)(2,1)} %pad_maximum_fusion.5) | data formatting | bytes 8388608 | tf_op jit(solution)/shard_map/concatenate | solution.py:251
  475.5 23.5 %collective-permute-done.55 = bf16[2,2,2,32,2304]{4,3,2,1,0:T(8,128)(2,1)S(1)} collective-permute-done((bf16[2,2,2,32,2304]{4,3,2,1,0:T(8,128)(2,1)S(1)}, bf16[2,2,2,32,2304]{4,3,2,1,0:T(8,128)(2,1)S(1)}, u32[]{:S(2)}, u32[]{:S(2)}) %collective-permute-start.55) | collective-permute-done | bytes 1179680 | tf_op jit(solution)/shard_map/ppermute | solution.py:27
  502.3 20.5 %collective-permute-done.56 = bf16[2,2,32,2304]{3,2,1,0:T(8,128)(2,1)S(1)} collective-permute-done((bf16[2,2,32,2304]{3,2,1,0:T(8,128)(2,1)S(1)}, bf16[2,2,32,2304]{3,2,1,0:T(8,128)(2,1)S(1)}, u32[]{:S(2)}, u32[]{:S(2)}) %collective-permute-start.56) | collective-permute-done | bytes 589856 | tf_op jit(solution)/shard_map/ppermute | solution.py:27
  523.5 14.9 %collective-permute-done.51 = bf16[2,2,32,2304]{3,2,1,0:T(8,128)(2,1)S(1)} collective-permute-done((bf16[2,2,32,2304]{3,2,1,0:T(8,128)(2,1)S(1)}, bf16[2,2,32,2304]{3,2,1,0:T(8,128)(2,1)S(1)}, u32[]{:S(2)}, u32[]{:S(2)}) %collective-permute-start.51) | collective-permute-done | bytes 589856 | tf_op jit(solution)/shard_map/ppermute | solution.py:27
  559.4 6.2 %collective-permute-done.45 = bf16[2,2,2,32,2048]{4,3,2,1,0:T(8,128)(2,1)} collective-permute-done((bf16[2,2,2,32,2048]{4,3,2,1,0:T(8,128)(2,1)}, bf16[2,2,2,32,2048]{4,3,2,1,0:T(8,128)(2,1)}, u32[]{:S(2)}, u32[]{:S(2)}) %collective-permute-start.45) | collective-permute-done | bytes 1048608 | tf_op jit(solution)/shard_map/ppermute | solution.py:27
  571.0 5.5 collective-permute-done.46
  581.6 4.8 collective-permute-done.47
  586.6 6.1 %collective-permute-done.42 = bf16[2,32,2048]{2,1,0:T(8,128)(2,1)S(1)} collective-permute-done((bf16[2,32,2048]{2,1,0:T(8,128)(2,1)S(1)}, bf16[2,32,2048]{2,1,0:T(8,128)(2,1)S(1)}, u32[]{:S(2)}, u32[]{:S(2)}) %collective-permute-start.42) | collective-permute-done | bytes 262176 | tf_op jit(solution)/shard_map/ppermute | solution.py:27
  (415 shorter events, 190.6 us)
Async XLA Ops:
  24.9 161.5 %collective-permute-start.31 = (bf16[512,1024]{1,0:T(8,128)(2,1)}, bf16[512,1024]{1,0:T(8,128)(2,1)}, u32[]{:S(2)}, u32[]{:S(2)}) collective-permute-start(bf16[512,1024]{1,0:T(8,128)(2,1)} %bitcast.83), channel_id=1, source_target_pairs={{0,2},{2,0},{4,6},{6,4},{8,10},{10,8},{12,14},{14,12},{16,18},{18,... | collective-permute-start | bytes 3145736 | tf_op jit(solution)/shard_map/ppermute | solution.py:27
  29.3 26.8 %collective-permute-start.13 = (bf16[2,32,2304]{2,1,0:T(8,128)(2,1)S(1)}, bf16[2,32,2304]{2,1,0:T(8,128)(2,1)S(1)}, u32[]{:S(2)}, u32[]{:S(2)}) collective-permute-start(bf16[2,32,2304]{2,1,0:T(8,128)(2,1)S(1)} %pad_maximum_fusion.37), channel_id=1, source_target_pairs={{0,8},{2,10},{4,12},{6,14},{8,0},{10,2},{12,4},{14,6},{16,24},{18,... | collective-permute-start | bytes 884744 | tf_op jit(solution)/shard_map/ppermute | solution.py:27
  30.0 27.7 %collective-permute-start.18 = (bf16[2,32,2304]{2,1,0:T(8,128)(2,1)S(1)}, bf16[2,32,2304]{2,1,0:T(8,128)(2,1)S(1)}, u32[]{:S(2)}, u32[]{:S(2)}) collective-permute-start(bf16[2,32,2304]{2,1,0:T(8,128)(2,1)S(1)} %pad_maximum_fusion.38), channel_id=1, source_target_pairs={{0,16},{2,18},{4,20},{6,22},{8,24},{10,26},{12,28},{14,30},{16,0},... | collective-permute-start | bytes 884744 | tf_op jit(solution)/shard_map/ppermute | solution.py:27
  66.7 28.5 %collective-permute-start.14 = (bf16[2,2,32,2304]{3,2,1,0:T(8,128)(2,1)S(1)}, bf16[2,2,32,2304]{3,2,1,0:T(8,128)(2,1)S(1)}, u32[]{:S(2)}, u32[]{:S(2)}) collective-permute-start(bf16[2,2,32,2304]{3,2,1,0:T(8,128)(2,1)S(1)} %pad_maximum_fusion.29), channel_id=1, source_target_pairs={{0,16},{2,18},{4,20},{6,22},{8,24},{10,26},{12,28},{14,30},{16,0},... | collective-permute-start | bytes 1769480 | tf_op jit(solution)/shard_map/ppermute | solution.py:27
  66.9 30.0 %collective-permute-start.19 = (bf16[2,2,32,2304]{3,2,1,0:T(8,128)(2,1)S(1)}, bf16[2,2,32,2304]{3,2,1,0:T(8,128)(2,1)S(1)}, u32[]{:S(2)}, u32[]{:S(2)}) collective-permute-start(bf16[2,2,32,2304]{3,2,1,0:T(8,128)(2,1)S(1)} %pad_maximum_fusion.30), channel_id=1, source_target_pairs={{0,8},{2,10},{4,12},{6,14},{8,0},{10,2},{12,4},{14,6},{16,24},{18,... | collective-permute-start | bytes 1769480 | tf_op jit(solution)/shard_map/ppermute | solution.py:27
  70.0 28.6 %collective-permute-start.24 = (bf16[2,2,144,512]{3,2,1,0:T(8,128)(2,1)S(1)}, bf16[2,2,144,512]{3,2,1,0:T(8,128)(2,1)S(1)}, u32[]{:S(2)}, u32[]{:S(2)}) collective-permute-start(bf16[2,2,144,512]{3,2,1,0:T(8,128)(2,1)S(1)} %pad_maximum_fusion.31), channel_id=1, source_target_pairs={{0,4},{2,6},{4,0},{6,2},{8,12},{10,14},{12,8},{14,10},{16,20},{18,... | collective-permute-start | bytes 1769480 | tf_op jit(solution)/shard_map/ppermute | solution.py:27
  72.0 27.4 %collective-permute-start.28 = (bf16[2,2,144,512]{3,2,1,0:T(8,128)(2,1)S(1)}, bf16[2,2,144,512]{3,2,1,0:T(8,128)(2,1)S(1)}, u32[]{:S(2)}, u32[]{:S(2)}) collective-permute-start(bf16[2,2,144,512]{3,2,1,0:T(8,128)(2,1)S(1)} %pad_maximum_fusion.32), channel_id=1, source_target_pairs={{0,1},{1,0},{2,3},{3,2},{4,5},{5,4},{6,7},{7,6},{8,9},{9,8},{10,11... | collective-permute-start | bytes 1769480 | tf_op jit(solution)/shard_map/ppermute | solution.py:27
  97.0 27.6 %collective-permute-start.3 = (bf16[2,2,2,32,2176]{4,3,2,1,0:T(8,128)(2,1)S(1)}, bf16[2,2,2,32,2176]{4,3,2,1,0:T(8,128)(2,1)S(1)}, u32[]{:S(2)}, u32[]{:S(2)}) collective-permute-start(bf16[2,2,2,32,2176]{4,3,2,1,0:T(8,128)(2,1)S(1)} %pad_maximum_fusion.25), channel_id=1, source_target_pairs={{0,4},{2,6},{4,0},{6,2},{8,12},{10,14},{12,8},{14,10},{16,20},{18,... | collective-permute-start | bytes 3342344 | tf_op jit(solution)/shard_map/ppermute | solution.py:27
  98.7 51.2 %collective-permute-start.15 = (bf16[2,2,2,32,2304]{4,3,2,1,0:T(8,128)(2,1)S(1)}, bf16[2,2,2,32,2304]{4,3,2,1,0:T(8,128)(2,1)S(1)}, u32[]{:S(2)}, u32[]{:S(2)}) collective-permute-start(bf16[2,2,2,32,2304]{4,3,2,1,0:T(8,128)(2,1)S(1)} %pad_maximum_fusion.21), channel_id=1, source_target_pairs={{0,4},{2,6},{4,0},{6,2},{8,12},{10,14},{12,8},{14,10},{16,20},{18,... | collective-permute-start | bytes 3538952 | tf_op jit(solution)/shard_map/ppermute | solution.py:27
  99.5 50.5 %collective-permute-start.20 = (bf16[2,2,2,32,2304]{4,3,2,0,1:T(8,128)(2,1)S(1)}, bf16[2,2,2,32,2304]{4,3,2,0,1:T(8,128)(2,1)S(1)}, u32[]{:S(2)}, u32[]{:S(2)}) collective-permute-start(bf16[2,2,2,32,2304]{4,3,2,0,1:T(8,128)(2,1)S(1)} %pad_maximum_fusion.22), channel_id=1, source_target_pairs={{0,1},{1,0},{2,3},{3,2},{4,5},{5,4},{6,7},{7,6},{8,9},{9,8},{10,11... | collective-permute-start | bytes 3538952 | tf_op jit(solution)/shard_map/ppermute | solution.py:27
  121.3 49.5 %collective-permute-start.25 = (bf16[2,2,2,144,512]{4,3,2,1,0:T(8,128)(2,1)S(1)}, bf16[2,2,2,144,512]{4,3,2,1,0:T(8,128)(2,1)S(1)}, u32[]{:S(2)}, u32[]{:S(2)}) collective-permute-start(bf16[2,2,2,144,512]{4,3,2,1,0:T(8,128)(2,1)S(1)} %pad_maximum_fusion.23), channel_id=1, source_target_pairs={{0,1},{1,0},{2,3},{3,2},{4,5},{5,4},{6,7},{7,6},{8,9},{9,8},{10,11... | collective-permute-start | bytes 3538952 | tf_op jit(solution)/shard_map/ppermute | solution.py:27
  124.6 49.8 %collective-permute-start.29 = (bf16[2,2,2,144,512]{4,3,2,1,0:T(8,128)(2,1)S(1)}, bf16[2,2,2,144,512]{4,3,2,1,0:T(8,128)(2,1)S(1)}, u32[]{:S(2)}, u32[]{:S(2)}) collective-permute-start(bf16[2,2,2,144,512]{4,3,2,1,0:T(8,128)(2,1)S(1)} %pad_maximum_fusion.24), channel_id=1, source_target_pairs={{0,4},{2,6},{4,0},{6,2},{8,12},{10,14},{12,8},{14,10},{16,20},{18,... | collective-permute-start | bytes 3538952 | tf_op jit(solution)/shard_map/ppermute | solution.py:27
  150.0 27.0 %collective-permute-start.4 = (bf16[2,2,2,2,32,2176]{5,4,3,2,1,0:T(8,128)(2,1)S(1)}, bf16[2,2,2,2,32,2176]{5,4,3,2,1,0:T(8,128)(2,1)S(1)}, u32[]{:S(2)}, u32[]{:S(2)}) collective-permute-start(bf16[2,2,2,2,32,2176]{5,4,3,2,1,0:T(8,128)(2,1)S(1)} %pad_maximum_fusion.12), channel_id=1, source_target_pairs={{0,2},{2,0},{4,6},{6,4},{8,10},{10,8},{12,14},{14,12},{16,18},{18,... | collective-permute-start | bytes 6684680 | tf_op jit(solution)/shard_map/ppermute | solution.py:27
  170.8 55.6 %collective-permute-start.16 = (bf16[2,2,2,2,32,2304]{5,4,3,1,0,2:T(8,128)(2,1)}, bf16[2,2,2,2,32,2304]{5,4,3,1,0,2:T(8,128)(2,1)}, u32[]{:S(2)}, u32[]{:S(2)}) collective-permute-start(bf16[2,2,2,2,32,2304]{5,4,3,1,0,2:T(8,128)(2,1)} %pad_maximum_fusion.8), channel_id=1, source_target_pairs={{0,1},{1,0},{2,3},{3,2},{4,5},{5,4},{6,7},{7,6},{8,9},{9,8},{10,11... | collective-permute-start | bytes 7077896 | tf_op jit(solution)/shard_map/ppermute | solution.py:27
  174.4 57.3 %collective-permute-start.21 = (bf16[2,2,2,2,32,2304]{5,4,2,0,1,3:T(8,128)(2,1)}, bf16[2,2,2,2,32,2304]{5,4,2,0,1,3:T(8,128)(2,1)}, u32[]{:S(2)}, u32[]{:S(2)}) collective-permute-start(bf16[2,2,2,2,32,2304]{5,4,2,0,1,3:T(8,128)(2,1)} %pad_maximum_fusion.9), channel_id=1, source_target_pairs={{0,4},{2,6},{4,0},{6,2},{8,12},{10,14},{12,8},{14,10},{16,20},{18,... | collective-permute-start | bytes 7077896 | tf_op jit(solution)/shard_map/ppermute | solution.py:27
  183.6 38.6 %collective-permute-start.10 = (bf16[1,2,1024]{2,1,0:T(2,128)(2,1)S(1)}, bf16[1,2,1024]{2,1,0:T(2,128)(2,1)S(1)}, u32[]{:S(2)}, u32[]{:S(2)}) collective-permute-start(bf16[1,2,1024]{2,1,0:T(2,128)(2,1)S(1)} %slice.152), channel_id=1, source_target_pairs={{0,1},{2,3},{4,5},{6,7},{8,9},{10,11},{12,13},{14,15},{16,17},{18,... | collective-permute-start | bytes 12296 | tf_op jit(solution)/shard_map/ppermute | solution.py:13
  278.5 45.3 %collective-permute-start.59 = (bf16[2,2,2,144,512]{4,3,1,0,2:T(8,128)(2,1)}, bf16[2,2,2,144,512]{4,3,1,0,2:T(8,128)(2,1)S(1)}, u32[]{:S(2)}, u32[]{:S(2)}) collective-permute-start(bf16[2,2,2,144,512]{4,3,1,0,2:T(8,128)(2,1)} %bitcast.381), channel_id=1, source_target_pairs={{0,1},{1,0},{2,3},{3,2},{4,5},{5,4},{6,7},{7,6},{8,9},{9,8},{10,11... | collective-permute-start | bytes 3538952 | tf_op jit(solution)/shard_map/ppermute | solution.py:27
  282.3 42.8 %collective-permute-start.63 = (bf16[2,2,2,144,512]{4,3,0,1,2:T(8,128)(2,1)}, bf16[2,2,2,144,512]{4,3,0,1,2:T(8,128)(2,1)S(1)}, u32[]{:S(2)}, u32[]{:S(2)}) collective-permute-start(bf16[2,2,2,144,512]{4,3,0,1,2:T(8,128)(2,1)} %bitcast.380), channel_id=1, source_target_pairs={{0,4},{2,6},{4,0},{6,2},{8,12},{10,14},{12,8},{14,10},{16,20},{18,... | collective-permute-start | bytes 3538952 | tf_op jit(solution)/shard_map/ppermute | solution.py:27
  304.4 163.5 %collective-permute-start.54 = (bf16[2,2,2,2,32,2304]{5,4,3,2,1,0:T(8,128)(2,1)}, bf16[2,2,2,2,32,2304]{5,4,3,2,1,0:T(8,128)(2,1)}, u32[]{:S(2)}, u32[]{:S(2)}) collective-permute-start(bf16[2,2,2,2,32,2304]{5,4,3,2,1,0:T(8,128)(2,1)} %dynamic-slice_bitcast_fusion), channel_id=1, source_target_pairs={{0,4},{2,6},{4,0},{6,2},{8,12},{10,14},{12,8},{14,10},{16,20},{18,... | collective-permute-start | bytes 7077896 | tf_op jit(solution)/shard_map/ppermute | solution.py:27
  305.7 96.0 %collective-permute-start.30 = (f32[512,1024]{1,0:T(8,128)S(1)}, f32[512,1024]{1,0:T(8,128)S(1)}, u32[]{:S(2)}, u32[]{:S(2)}) collective-permute-start(f32[512,1024]{1,0:T(8,128)S(1)} %slice.161), channel_id=1, source_target_pairs={{0,2},{2,0},{4,6},{6,4},{8,10},{10,8},{12,14},{14,12},{16,18},{18,... | collective-permute-start | bytes 6291464 | tf_op jit(solution)/shard_map/ppermute | solution.py:27
  314.2 83.9 %collective-permute-start.32 = (f32[512,1024]{1,0:T(8,128)S(1)}, f32[512,1024]{1,0:T(8,128)S(1)}, u32[]{:S(2)}, u32[]{:S(2)}) collective-permute-start(f32[512,1024]{1,0:T(8,128)S(1)} %slice.163), channel_id=1, source_target_pairs={{0,2},{2,0},{4,6},{6,4},{8,10},{10,8},{12,14},{14,12},{16,18},{18,... | collective-permute-start | bytes 6291464 | tf_op jit(solution)/shard_map/ppermute | solution.py:27
  324.2 49.3 %collective-permute-start.60 = (bf16[2,2,144,512]{3,2,1,0:T(8,128)(2,1)S(1)}, bf16[2,2,144,512]{3,2,1,0:T(8,128)(2,1)S(1)}, u32[]{:S(2)}, u32[]{:S(2)}) collective-permute-start(bf16[2,2,144,512]{3,2,1,0:T(8,128)(2,1)S(1)} %dynamic-slice_bitcast_fusion.8), channel_id=1, source_target_pairs={{0,4},{2,6},{4,0},{6,2},{8,12},{10,14},{12,8},{14,10},{16,20},{18,... | collective-permute-start | bytes 1769480 | tf_op jit(solution)/shard_map/ppermute | solution.py:27
  325.5 48.5 %collective-permute-start.64 = (bf16[2,2,144,512]{3,2,0,1:T(8,128)(2,1)S(1)}, bf16[2,2,144,512]{3,2,0,1:T(8,128)(2,1)S(1)}, u32[]{:S(2)}, u32[]{:S(2)}) collective-permute-start(bf16[2,2,144,512]{3,2,0,1:T(8,128)(2,1)S(1)} %dynamic-slice_bitcast_fusion.7), channel_id=1, source_target_pairs={{0,1},{1,0},{2,3},{3,2},{4,5},{5,4},{6,7},{7,6},{8,9},{9,8},{10,11... | collective-permute-start | bytes 1769480 | tf_op jit(solution)/shard_map/ppermute | solution.py:27
  373.5 98.1 %collective-permute-start.49 = (bf16[2,2,2,2,32,2304]{5,4,3,2,1,0:T(8,128)(2,1)}, bf16[2,2,2,2,32,2304]{5,4,3,2,1,0:T(8,128)(2,1)}, u32[]{:S(2)}, u32[]{:S(2)}) collective-permute-start(bf16[2,2,2,2,32,2304]{5,4,3,2,1,0:T(8,128)(2,1)} %dynamic-slice_bitcast_fusion.1), channel_id=1, source_target_pairs={{0,1},{1,0},{2,3},{3,2},{4,5},{5,4},{6,7},{7,6},{8,9},{9,8},{10,11... | collective-permute-start | bytes 7077896 | tf_op jit(solution)/shard_map/ppermute | solution.py:27
  397.0 68.4 %collective-permute-start.62 = (bf16[144,512]{1,0:T(8,128)(2,1)}, bf16[144,512]{1,0:T(8,128)(2,1)}, u32[]{:S(2)}, u32[]{:S(2)}) collective-permute-start(bf16[144,512]{1,0:T(8,128)(2,1)} %dynamic-slice_bitcast_fusion.22), channel_id=1, source_target_pairs={{0,8},{2,10},{4,12},{6,14},{8,0},{10,2},{12,4},{14,6},{16,24},{18,... | collective-permute-start | bytes 442376 | tf_op jit(solution)/shard_map/ppermute | solution.py:27
  398.2 68.7 %collective-permute-start.66 = (bf16[144,512]{1,0:T(8,128)(2,1)}, bf16[144,512]{1,0:T(8,128)(2,1)}, u32[]{:S(2)}, u32[]{:S(2)}) collective-permute-start(bf16[144,512]{1,0:T(8,128)(2,1)} %dynamic-slice_bitcast_fusion.21), channel_id=1, source_target_pairs={{0,16},{2,18},{4,20},{6,22},{8,24},{10,26},{12,28},{14,30},{16,0},... | collective-permute-start | bytes 442376 | tf_op jit(solution)/shard_map/ppermute | solution.py:27
  464.2 75.0 %collective-permute-start.39 = (bf16[2,2,2,2,32,2048]{5,4,1,0,2,3:T(8,128)(2,1)S(1)}, bf16[2,2,2,2,32,2048]{5,4,1,0,2,3:T(8,128)(2,1)S(1)}, u32[]{:S(2)}, u32[]{:S(2)}) collective-permute-start(bf16[2,2,2,2,32,2048]{5,4,1,0,2,3:T(8,128)(2,1)S(1)} %bitcast.421), channel_id=1, source_target_pairs={{0,2},{2,0},{4,6},{6,4},{8,10},{10,8},{12,14},{14,12},{16,18},{18,... | collective-permute-start | bytes 6291464 | tf_op jit(solution)/shard_map/ppermute | solution.py:27
  465.4 77.1 %collective-permute-start.44 = (bf16[2,2,2,2,32,2048]{5,4,3,2,1,0:T(8,128)(2,1)S(1)}, bf16[2,2,2,2,32,2048]{5,4,3,2,1,0:T(8,128)(2,1)S(1)}, u32[]{:S(2)}, u32[]{:S(2)}) collective-permute-start(bf16[2,2,2,2,32,2048]{5,4,3,2,1,0:T(8,128)(2,1)S(1)} %dynamic-slice_bitcast_fusion.2), channel_id=1, source_target_pairs={{0,2},{2,0},{4,6},{6,4},{8,10},{10,8},{12,14},{14,12},{16,18},{18,... | collective-permute-start | bytes 6291464 | tf_op jit(solution)/shard_map/ppermute | solution.py:27
  471.0 27.9 %collective-permute-start.55 = (bf16[2,2,2,32,2304]{4,3,2,1,0:T(8,128)(2,1)S(1)}, bf16[2,2,2,32,2304]{4,3,2,1,0:T(8,128)(2,1)S(1)}, u32[]{:S(2)}, u32[]{:S(2)}) collective-permute-start(bf16[2,2,2,32,2304]{4,3,2,1,0:T(8,128)(2,1)S(1)} %dynamic-slice_bitcast_fusion.3), channel_id=1, source_target_pairs={{0,1},{1,0},{2,3},{3,2},{4,5},{5,4},{6,7},{7,6},{8,9},{9,8},{10,11... | collective-permute-start | bytes 3538952 | tf_op jit(solution)/shard_map/ppermute | solution.py:27
  474.0 27.7 %collective-permute-start.50 = (bf16[2,2,2,32,2304]{4,3,2,1,0:T(8,128)(2,1)S(1)}, bf16[2,2,2,32,2304]{4,3,2,1,0:T(8,128)(2,1)S(1)}, u32[]{:S(2)}, u32[]{:S(2)}) collective-permute-start(bf16[2,2,2,32,2304]{4,3,2,1,0:T(8,128)(2,1)S(1)} %dynamic-slice_bitcast_fusion.4), channel_id=1, source_target_pairs={{0,4},{2,6},{4,0},{6,2},{8,12},{10,14},{12,8},{14,10},{16,20},{18,... | collective-permute-start | bytes 3538952 | tf_op jit(solution)/shard_map/ppermute | solution.py:27
  502.1 36.2 %collective-permute-start.51 = (bf16[2,2,32,2304]{3,2,1,0:T(8,128)(2,1)S(1)}, bf16[2,2,32,2304]{3,2,1,0:T(8,128)(2,1)S(1)}, u32[]{:S(2)}, u32[]{:S(2)}) collective-permute-start(bf16[2,2,32,2304]{3,2,1,0:T(8,128)(2,1)S(1)} %dynamic-slice_bitcast_fusion.10), channel_id=1, source_target_pairs={{0,16},{2,18},{4,20},{6,22},{8,24},{10,26},{12,28},{14,30},{16,0},... | collective-permute-start | bytes 1769480 | tf_op jit(solution)/shard_map/ppermute | solution.py:27
  541.1 27.6 %collective-permute-start.40 = (bf16[2,2,2,32,2048]{4,3,1,0,2:T(8,128)(2,1)}, bf16[2,2,2,32,2048]{4,3,1,0,2:T(8,128)(2,1)}, u32[]{:S(2)}, u32[]{:S(2)}) collective-permute-start(bf16[2,2,2,32,2048]{4,3,1,0,2:T(8,128)(2,1)} %dynamic-slice_bitcast_fusion.6), channel_id=1, source_target_pairs={{0,1},{1,0},{2,3},{3,2},{4,5},{5,4},{6,7},{7,6},{8,9},{9,8},{10,11... | collective-permute-start | bytes 3145736 | tf_op jit(solution)/shard_map/ppermute | solution.py:27
  (94 other events, 1191.9 us)

commit v2 on v0

v2 whole, which is shorter than its diff:
```python
import jax
import jax.numpy as jnp
from jax import lax
from jax.sharding import PartitionSpec as P

EPSILON = 1e-05
CORE = ("fsdp", 0)
SIDE = ("seq", 0)


def shifted(shard, axis, by):
    size = lax.axis_size(axis)
    pairs = [(i, i + by) for i in range(size) if 0 <= i + by < size]
    return lax.ppermute(shard, axis, pairs)


def bit_count(axis):
    return lax.axis_size(axis).bit_length() - 1


def my_bit(dim):
    axis, bit = dim
    return (lax.axis_index(axis) >> bit) & 1


def swap(value, dim):
    axis, bit = dim
    return lax.ppermute(value, axis, [(i, i ^ (1 << bit)) for i in range(lax.axis_size(axis))])


def rank(dim):
    axis, bit = dim
    return (0 if axis == "fsdp" else 1, -bit)


def down_rank(dim):
    top = bit_count("fsdp") - 1
    return rank({("fsdp", top): CORE, ("fsdp", top - 1): SIDE}.get(dim, dim))


def tie(*values):
    return lax.optimization_barrier(values)


class Gather:
    def __init__(self, piece, dims, held=(), order=rank):
        self.buffer, self.left, self.held, self.order = piece, list(dims), list(held), order

    def step(self):
        if not self.left:
            return
        dim = self.left.pop(0)
        other, mine = swap(self.buffer, dim), self.buffer
        axis = sum(self.order(h) < self.order(dim) for h in self.held)
        high = my_bit(dim) == 1
        self.buffer = jnp.stack(
            [jnp.where(high, other, mine), jnp.where(high, mine, other)], axis=axis
        )
        self.held.append(dim)


class Scatter:
    def __init__(self, terms, dims, held, order=rank):
        self.buffer, self.left, self.order = terms, list(dims), order
        self.held = sorted(held, key=order)

    def step(self):
        if not self.left:
            return
        dim = self.left.pop(0)
        axis = self.held.index(dim)
        bit = my_bit(dim)
        keep = lax.dynamic_index_in_dim(self.buffer, bit, axis, keepdims=False)
        send = lax.dynamic_index_in_dim(self.buffer, 1 - bit, axis, keepdims=False)
        total = keep.astype(jnp.float32) + swap(send, dim).astype(jnp.float32)
        self.buffer = total.astype(jnp.bfloat16) if self.left else total
        self.held.remove(dim)


def advance(chains, *others):
    for chain in chains:
        chain.step()
    tied = tie(*(chain.buffer for chain in chains), *others)
    for chain, buffer in zip(chains, tied):
        chain.buffer = buffer
    return tied[len(chains) :]


def finish(*chains):
    for chain in chains:
        while chain.left:
            chain.step()


def normalize(values, gain):
    scale = lax.rsqrt(jnp.mean(values * values, axis=-1, keepdims=True) + EPSILON)
    normalized_rows = values * scale
    return (normalized_rows, scale, normalized_rows * gain)


def norm_back(d_hidden, normalized_rows, scale, gain):
    norm_gradient = d_hidden * gain
    grad_gain = jnp.sum(d_hidden * normalized_rows, axis=0)
    d_input = scale * (
        norm_gradient
        - normalized_rows * jnp.mean(norm_gradient * normalized_rows, axis=-1, keepdims=True)
    )
    return (d_input, grad_gain)


def dot_plain(left_segment, right_segment):
    return jnp.dot(left_segment, right_segment, preferred_element_type=jnp.float32)


def dot_first(left_segment, right_segment):
    return lax.dot_general(
        left_segment, right_segment, (((0,), (0,)), ((), ())), preferred_element_type=jnp.float32
    )


def dot_second(left_segment, right_segment):
    return lax.dot_general(
        left_segment, right_segment, (((1,), (1,)), ((), ())), preferred_element_type=jnp.float32
    )


def quarter_owner_swap(value):
    fsdp, seq = lax.axis_size("fsdp"), lax.axis_size("seq")
    top = bit_count("fsdp") - 1
    pairs = []
    for device in range(fsdp * seq):
        f, s = divmod(device, seq)
        high, low = (f >> top) & 1, (f >> (top - 1)) & 1
        core, side = f & 1, s & 1
        f2 = (f & ~((1 << top) | (1 << (top - 1)) | 1)) | (core << top) | (side << (top - 1)) | high
        pairs.append((device, f2 * seq + ((s & ~1) | low)))
    return lax.ppermute(value, ("fsdp", "seq"), pairs)


def body(tokens, gain_a, mix_in, conv_tap, mix_out, gain_b, ff_gate, ff_up, ff_down, cotangent):
    seq_count, local_rows, feature_width = tokens.shape
    row_total = seq_count * local_rows
    pair_rows = 2 * row_total
    tap_count = conv_tap.shape[0]
    own_rows = mix_in.shape[0]
    hidden_units = ff_gate.shape[1]
    quarter = hidden_units // 4
    core, side = my_bit(CORE), my_bit(SIDE)
    near = [("fsdp", 1)]
    far = [("fsdp", b) for b in range(2, bit_count("fsdp"))]
    outer = [("seq", b) for b in range(1, bit_count("seq"))]
    zx, zx_turned = far + near + outer, far[::-1] + near + outer
    route_a, route_b = far + near + outer + [SIDE], far[::-1] + [SIDE] + outer + near
    group = [CORE, SIDE]
    half_width = 2 * feature_width
    down_half = feature_width // 2

    def ordered(pair_bit, mine, other):
        high = pair_bit == 1
        return jnp.where(high, other, mine), jnp.where(high, mine, other)

    small = jnp.concatenate([gain_a[None], gain_b[None], conv_tap], axis=0).T
    small = jnp.pad(small, ((0, 0), (0, 128 - small.shape[1])))
    mix_a = Gather(
        jnp.concatenate([mix_in[:, :feature_width], mix_in[:, 2 * feature_width :]], axis=1), route_a
    )
    mix_b = Gather(
        jnp.concatenate([mix_in[:, feature_width : 2 * feature_width], mix_out, small], axis=1),
        route_b,
    )
    down_x = Gather(ff_down, near + outer)

    def quarters(shard):
        return jnp.stack([shard[:, q * quarter : (q + 1) * quarter] for q in range(4)]).reshape(
            2, 2, own_rows, quarter
        )

    def regroup(parts, axis, bit, dim):
        mine = lax.dynamic_index_in_dim(parts, bit, axis, keepdims=False)
        other = swap(lax.dynamic_index_in_dim(parts, 1 - bit, axis, keepdims=False), dim)
        return mine, other

    gate_mine, gate_other = regroup(quarters(ff_gate), 1, side, SIDE)
    up_mine, up_other = regroup(quarters(ff_up), 1, side, SIDE)
    cot_low = cotangent.reshape(row_total, feature_width)
    cot_first, cot_last = cot_low[: row_total // 2], cot_low[row_total // 2 :]
    gate_mine, gate_other, up_mine, up_other, cot_first = advance(
        [mix_a, mix_b, down_x], gate_mine, gate_other, up_mine, up_other, cot_first
    )

    def regroup_core(mine, other):
        both = jnp.stack(ordered(side, mine, other), axis=1)
        return jnp.stack(ordered(core, *regroup(both, 0, core, CORE)), axis=0)

    gate = Gather(regroup_core(gate_mine, gate_other), zx, group)
    up = Gather(regroup_core(up_mine, up_other), zx_turned, group)
    cot_first_other = swap(cot_first, SIDE)
    gate.buffer, up.buffer, cot_first_other, cot_last = advance(
        [mix_a, mix_b], gate.buffer, up.buffer, cot_first_other, cot_last
    )

    while mix_a.left or mix_b.left:
        advance([mix_a, mix_b, gate, up])

    inputs = tokens.reshape(row_total, feature_width).astype(jnp.float32)
    cot_full = cot_low.astype(jnp.float32)
    core_a, core_b = Gather(mix_a.buffer, [CORE], mix_a.held), Gather(mix_b.buffer, [CORE], mix_b.held)
    core_a.step()
    core_b.step()
    weight_bv = core_a.buffer.reshape(feature_width, half_width)
    weight_c_out = core_b.buffer.reshape(feature_width, half_width + 128)
    weight_c = weight_c_out[:, :feature_width]
    weight_out = weight_c_out[:, feature_width:half_width]
    small_whole = weight_c_out[:, half_width : half_width + 2 + tap_count].T.astype(jnp.float32)
    gain_one, gain_two, tap_values = small_whole[0], small_whole[1], small_whole[2:]
    normed_a, scale_a, hidden = normalize(inputs, gain_one)
    hidden_low = hidden.astype(jnp.bfloat16)
    bv_part = dot_plain(hidden_low, weight_bv)
    b_part = bv_part[:, :feature_width]
    v_part = bv_part[:, feature_width:]
    mixed = (b_part * v_part).astype(jnp.bfloat16).reshape(seq_count, local_rows, feature_width)
    edge_rows = shifted(mixed[:, local_rows - (tap_count - 1) :, :], "seq", 1)
    c_part = dot_plain(hidden_low, weight_c)
    edge_rows, cot_last = tie(edge_rows, cot_last)
    cot_last_other = swap(cot_last, SIDE)
    extended = jnp.concatenate([edge_rows, mixed], axis=1).astype(jnp.float32)
    convolved = tap_values[0] * extended[:, 0:local_rows]
    for offset in range(1, tap_count):
        convolved = convolved + tap_values[offset] * extended[:, offset : offset + local_rows]
    convolved = convolved.reshape(row_total, feature_width)
    gated = (c_part * convolved).astype(jnp.bfloat16)
    after_mix = inputs + dot_plain(gated, weight_out)
    normed_b, scale_b, hidden_b = normalize(after_mix, gain_two)
    hidden_b_low = hidden_b.astype(jnp.bfloat16)
    finish(down_x)
    down_piece = quarter_owner_swap(down_x.buffer)
    down_a = Gather(down_piece[..., :down_half], far, near + outer, down_rank)
    down_b = Gather(down_piece[..., down_half:], far[::-1], near + outer, down_rank)
    hidden_b_low, cot_last_other = advance(
        [gate, down_a, down_b], hidden_b_low, cot_last_other
    )
    finish(gate)

    hidden_two = jnp.concatenate([hidden_b_low, swap(hidden_b_low, SIDE)], axis=0)
    hidden_four = jnp.concatenate([hidden_two, swap(hidden_two, CORE)], axis=0)
    cot_two = jnp.concatenate([cot_low, cot_first_other, cot_last_other], axis=0)
    cot_four = jnp.concatenate([cot_two, swap(cot_two, CORE)], axis=0)
    hidden_four, cot_four = advance([up, down_a, down_b], hidden_four, cot_four)
    finish(up, down_a, down_b)
    weight_gate = gate.buffer.reshape(feature_width, quarter)
    weight_up = up.buffer.reshape(feature_width, quarter)
    weight_down = jnp.concatenate(
        [down_a.buffer.reshape(quarter, down_half), down_b.buffer.reshape(quarter, down_half)], axis=1
    )

    gate_value = dot_plain(hidden_four, weight_gate)
    up_value = dot_plain(hidden_four, weight_up)
    sigmoid_gate = jax.nn.sigmoid(gate_value)
    silu_gate = gate_value * sigmoid_gate
    active = (silu_gate * up_value).astype(jnp.bfloat16)

    def split(gradient, rows):
        return gradient.astype(jnp.bfloat16).reshape((2,) * len(zx) + rows)

    grad_down = split(dot_first(active, cot_four), (-1, feature_width))
    grad_down, cot_four = tie(grad_down, cot_four)
    grad_down_a = Scatter(grad_down[..., :down_half], zx[::-1], zx, down_rank)
    grad_down_b = Scatter(grad_down[..., down_half:], zx_turned[::-1], zx, down_rank)

    d_active = dot_second(cot_four, weight_down)
    d_up = (d_active * silu_gate).astype(jnp.bfloat16)
    d_gate = (
        d_active * up_value * sigmoid_gate * (1.0 + gate_value * (1.0 - sigmoid_gate))
    ).astype(jnp.bfloat16)

    def two_rows(parts):
        def rows(at):
            return sum(dot(left[at], right) for dot, left, right in parts)

        far_rows = rows(slice(pair_rows, None)).astype(jnp.bfloat16)
        two = rows(slice(0, pair_rows)) + swap(far_rows, CORE).astype(jnp.float32)
        return two[:row_total], two[row_total:].astype(jnp.bfloat16)

    d_hidden_own, d_hidden_far = two_rows(
        [(dot_second, d_gate, weight_gate), (dot_second, d_up, weight_up)]
    )
    d_hidden_own, d_hidden_far, d_gate, d_up = tie(d_hidden_own, d_hidden_far, d_gate, d_up)
    gate_rows = (2, 2, own_rows, quarter)
    grad_gate = Scatter(split(dot_first(hidden_four, d_gate), gate_rows), zx[::-1], zx + group)
    grad_gate.buffer, d_hidden_own, d_hidden_far, d_up, active = advance(
        [grad_down_a, grad_down_b], grad_gate.buffer, d_hidden_own, d_hidden_far, d_up, active
    )

    d_hidden_b = d_hidden_own + swap(d_hidden_far, SIDE).astype(jnp.float32)
    grad_up = Scatter(
        split(dot_first(hidden_four, d_up), gate_rows), zx_turned[::-1], zx + group
    )
    out_own, out_far = two_rows([(dot_plain, active, weight_down)])
    d_hidden_b, grad_up.buffer, out_own, out_far = advance(
        [grad_gate, grad_down_a, grad_down_b], d_hidden_b, grad_up.buffer, out_own, out_far
    )

    d_norm_input, grad_gain_two = norm_back(d_hidden_b, normed_b, scale_b, gain_two)
    d_after = cot_full + d_norm_input
    d_branch = d_after.astype(jnp.bfloat16)
    d_gated = dot_second(d_branch, weight_out)
    d_c = (d_gated * convolved).astype(jnp.bfloat16)
    d_conv = (d_gated * c_part).reshape(seq_count, local_rows, feature_width)
    padded_grad = jnp.pad(d_conv, ((0, 0), (tap_count - 1, tap_count - 1), (0, 0)))
    span = local_rows + tap_count - 1
    d_extended = tap_values[0] * padded_grad[:, tap_count - 1 : tap_count - 1 + span]
    for offset in range(1, tap_count):
        start_at = tap_count - 1 - offset
        d_extended = d_extended + tap_values[offset] * padded_grad[:, start_at : start_at + span]
    incoming = shifted(d_extended[:, : tap_count - 1, :], "seq", -1)
    incoming, out_far = tie(incoming, out_far)
    out_other = swap(out_far, SIDE).astype(jnp.float32)
    results = after_mix + (out_own + out_other)
    block_out = results.astype(jnp.bfloat16).reshape(seq_count, local_rows, feature_width)
    held_all = route_a + [CORE]
    shape_all = (2,) * len(held_all) + (own_rows, half_width)
    terms_b = jnp.concatenate(
        [
            dot_first(gated, d_branch).astype(jnp.bfloat16),
            dot_first(hidden_low, d_c).astype(jnp.bfloat16),
        ],
        axis=1,
    )
    grad_b = Scatter(terms_b.reshape(shape_all), [CORE] + route_b[::-1], held_all)
    grad_b.step()
    incoming_full = jnp.pad(incoming, ((0, 0), (local_rows - (tap_count - 1), 0), (0, 0)))
    d_mixed = (d_extended[:, tap_count - 1 :, :] + incoming_full).reshape(row_total, feature_width)
    d_bv = jnp.concatenate(
        [(d_mixed * v_part).astype(jnp.bfloat16), (d_mixed * b_part).astype(jnp.bfloat16)], axis=1
    )
    grad_a = Scatter(
        dot_first(hidden_low, d_bv).astype(jnp.bfloat16).reshape(shape_all),
        [CORE] + route_a[::-1],
        held_all,
    )
    grad_a.step()
    d_bv, d_c, d_conv, block_out, grad_a.buffer, grad_b.buffer = advance(
        [grad_up, grad_gate, grad_down_a, grad_down_b],
        d_bv, d_c, d_conv, block_out, grad_a.buffer, grad_b.buffer,
    )
    finish(grad_down_a, grad_down_b)
    down_owned = quarter_owner_swap(
        jnp.concatenate([grad_down_a.buffer, grad_down_b.buffer], axis=-1)
    )

    grad_taps = jnp.stack(
        [
            jnp.sum(d_conv * extended[:, offset : offset + local_rows], axis=(0, 1))
            for offset in range(tap_count)
        ],
        axis=0,
    )
    d_hidden = dot_second(d_bv, weight_bv) + dot_second(d_c, weight_c)
    d_first_norm, grad_gain_one = norm_back(d_hidden, normed_a, scale_a, gain_one)
    grad_tokens = (d_after + d_first_norm).reshape(seq_count, local_rows, feature_width)
    small_terms = jnp.concatenate(
        [grad_gain_one[None, :], grad_gain_two[None, :], grad_taps], axis=0
    )
    small_terms, grad_tokens, down_owned = advance(
        [grad_a, grad_b, grad_up, grad_gate], small_terms, grad_tokens, down_owned
    )
    finish(grad_gate)

    def owned_quarters(owned):
        both = jnp.stack(ordered(core, *regroup(owned, 0, core, CORE)), axis=1)
        mine = lax.dynamic_index_in_dim(both, side, 0, keepdims=False)
        send = lax.dynamic_index_in_dim(both, 1 - side, 0, keepdims=False)
        other = swap(send.astype(jnp.bfloat16), SIDE).astype(jnp.float32)
        low, high = ordered(side, mine, other)
        return jnp.concatenate([low[0], high[0], low[1], high[1]], axis=-1)

    gate_owned = owned_quarters(grad_gate.buffer)
    advance([grad_a, grad_b, grad_up])
    finish(grad_up)
    up_owned = owned_quarters(grad_up.buffer)
    for dim in [CORE] + route_a:
        small_terms = small_terms + swap(small_terms, dim)
    while grad_a.left or grad_b.left:
        advance([grad_a, grad_b])
    owned_a, owned_b = grad_a.buffer, grad_b.buffer
    place = lax.axis_index("fsdp") * lax.axis_size("seq") + lax.axis_index("seq")
    small_owned = lax.dynamic_slice_in_dim(small_terms, place * own_rows, own_rows, axis=1)
    return (
        block_out,
        grad_tokens,
        small_owned[0],
        jnp.concatenate(
            [owned_a[:, :feature_width], owned_b[:, feature_width:], owned_a[:, feature_width:]],
            axis=1,
        ),
        small_owned[2:],
        owned_b[:, :feature_width],
        small_owned[1],
        gate_owned,
        up_owned,
        down_owned,
    )


def solution(mesh):
    return jax.shard_map(
        body,
        mesh=mesh,
        in_specs=(
            P("fsdp", "seq", None),
            P(("fsdp", "seq")),
            P(("fsdp", "seq"), None),
            P(None, ("fsdp", "seq")),
            P(("fsdp", "seq"), None),
            P(("fsdp", "seq")),
            P(("fsdp", "seq"), None),
            P(("fsdp", "seq"), None),
            P(("fsdp", "seq"), None),
            P("fsdp", "seq", None),
        ),
        out_specs=(
            P("fsdp", "seq", None),
            P("fsdp", "seq", None),
            P(("fsdp", "seq")),
            P(("fsdp", "seq"), None),
            P(None, ("fsdp", "seq")),
            P(("fsdp", "seq"), None),
            P(("fsdp", "seq")),
            P(("fsdp", "seq"), None),
            P(("fsdp", "seq"), None),
            P(("fsdp", "seq"), None),
        ),
        check_vma=False,
    )
```

time: 1530 us -> 518 us (0.34)
  waiting for transfers between devices: 1230 us -> 238 us
  blocking collectives: 109 us -> 0 us
  starting transfers between devices: 3.01 us -> 83 us
  matrix products: 124 us -> 94.8 us
  local copies, waits for them, and re-layouts: 18.2 us -> 44.4 us
  other arithmetic: 22.9 us -> 45.8 us
    reduce_scatter x3 -> x0, waiting for transfers between devices: 917 us -> none  [the longest x1 354 us: body(): lax.psum_scatter(dot_first(hidden_b_low, gate_up_grads), ('fsdp', 'seq'),...]
    ppermute x0 -> x67, waiting for transfers between devices: none -> 237 us  [the longest x65 237 us: swap(): lax.ppermute(value, axis, [(i, i ^ 1 << bit) for i in range(lax.axis_size...]
    all_gather x5 -> x0, waiting for transfers between devices: 232 us -> none  [the longest x1 77.9 us: body(): lax.all_gather(ff_up, ('fsdp', 'seq'), axis=0, tiled=True)]
    ppermute x0 -> x67, starting transfers between devices: none -> 76.8 us  [the longest x65 70 us: swap(): lax.ppermute(value, axis, [(i, i ^ 1 << bit) for i in range(lax.axis_size...]
    unnamed x10 -> x0, waiting for transfers between devices: 75 us -> none
    all_gather x1 -> x0, blocking collectives: 66.8 us -> none  [body(): lax.all_gather(conv_tap, ('fsdp', 'seq'), axis=1, tiled=True)]
    unnamed x1 -> x0, blocking collectives: 42.2 us -> none
    dot_general x4 -> x6, matrix products: 43.2 us -> 22.9 us  [dot_first(): lax.dot_general(left_segment, right_segment, (((0,), (0,)), ((), ())), pr...]
  transfers between devices with their start and end apart: 11 -> 69, of which waited for: 10 -> 37; matrix products, arithmetic and copies ran while one was open for 7% -> 17% of each run, Pallas kernels for 0% -> 0%
where the time goes in v2:
time: 518 us; the launch traced here: 509 us
  waiting for transfers between devices  238 us (46%)
  matrix products  94.8 us (18%)
  starting transfers between devices  83 us (16%)
  other arithmetic  45.8 us (9%)
  local copies, waits for them, and re-layouts  44.4 us (9%)
    ppermute x65, waiting for transfers between devices, swap(): lax.ppermute(value, axis, [(i, i ^ 1 << bit) for i in range(lax.axis_size...  237 us
    ppermute x65, starting transfers between devices, swap(): lax.ppermute(value, axis, [(i, i ^ 1 << bit) for i in range(lax.axis_size...  70 us
    dot_general x8, matrix products, dot_second(): lax.dot_general(left_segment, right_segment, (((1,), (1,)), ((), ())), pr...  40.1 us
    dot_general x7, matrix products, dot_plain(): jnp.dot(left_segment, right_segment, preferred_element_type=jnp.float32)  31.8 us
    dot_general x6, matrix products, dot_first(): lax.dot_general(left_segment, right_segment, (((0,), (0,)), ((), ())), pr...  22.9 us
    unnamed x147, local copies, waits for them, and re-layouts  17 us
    convert_element_type x16, other arithmetic, step(): self.buffer = total.astype(jnp.bfloat16) if self.left else total  12 us
  transfers between devices with their start and end apart: 69, of which 37 were waited for; matrix products, arithmetic and copies ran while one was open for 17% of the time, Pallas kernels for 0%

profile of v2, /device:TPU:0, one launch (start us, length us, event | category | flops | bytes accessed | tf_op | source)
XLA Modules:
  0.0 508.8 jit_solution(852991295922116602)
XLA Ops:
  25.1 9.6 %collective-permute-done.5 = bf16[2,32,2048]{2,1,0:T(8,128)(2,1)S(1)} collective-permute-done((bf16[2,32,2048]{2,1,0:T(8,128)(2,1)S(1)}, bf16[2,32,2048]{2,1,0:T(8,128)(2,1)S(1)}, u32[]{:S(2)}, u32[]{:S(2)}) %collective-permute-start.5) | collective-permute-done | bytes 262176 | tf_op jit(solution)/shard_map/ppermute | solution.py:28
  43.5 7.4 %collective-permute-done.12 = bf16[2,2,32,1152]{3,2,1,0:T(8,128)(2,1)S(1)} collective-permute-done((bf16[2,2,32,1152]{3,2,1,0:T(8,128)(2,1)S(1)}, bf16[2,2,32,1152]{3,2,1,0:T(8,128)(2,1)S(1)}, u32[]{:S(2)}, u32[]{:S(2)}) %collective-permute-start.12) | collective-permute-done | bytes 294944 | tf_op jit(solution)/shard_map/ppermute | solution.py:28
  51.0 5.3 %collective-permute-done.13 = bf16[2,2,32,1152]{3,2,1,0:T(8,128)(2,1)S(1)} collective-permute-done((bf16[2,2,32,1152]{3,2,1,0:T(8,128)(2,1)S(1)}, bf16[2,2,32,1152]{3,2,1,0:T(8,128)(2,1)S(1)}, u32[]{:S(2)}, u32[]{:S(2)}) %collective-permute-start.13) | collective-permute-done | bytes 294944 | tf_op jit(solution)/shard_map/ppermute | solution.py:28
  57.1 11.9 %collective-permute-start.17 = (bf16[2,2,2,32,1152]{4,3,2,1,0:T(8,128)(2,1)S(1)}, bf16[2,2,2,32,1152]{4,3,2,1,0:T(8,128)(2,1)S(1)}, u32[]{:S(2)}, u32[]{:S(2)}) collective-permute-start(bf16[2,2,2,32,1152]{4,3,2,1,0:T(8,128)(2,1)S(1)} %pad_maximum_fusion.24), channel_id=1, source_target_pairs={{0,8},{2,10},{4,12},{6,14},{8,0},{10,2},{12,4},{14,6},{16,24},{18,... | collective-permute-start | bytes 1769480 | tf_op jit(solution)/shard_map/ppermute | solution.py:28
  72.5 6.4 %collective-permute-done.16 = bf16[2,2,2,32,1152]{4,3,2,1,0:T(8,128)(2,1)S(1)} collective-permute-done((bf16[2,2,2,32,1152]{4,3,2,1,0:T(8,128)(2,1)S(1)}, bf16[2,2,2,32,1152]{4,3,2,1,0:T(8,128)(2,1)S(1)}, u32[]{:S(2)}, u32[]{:S(2)}) %collective-permute-start.16) | collective-permute-done | bytes 589856 | tf_op jit(solution)/shard_map/ppermute | solution.py:28
  79.0 8.4 %collective-permute-done.17 = bf16[2,2,2,32,1152]{4,3,2,1,0:T(8,128)(2,1)S(1)} collective-permute-done((bf16[2,2,2,32,1152]{4,3,2,1,0:T(8,128)(2,1)S(1)}, bf16[2,2,2,32,1152]{4,3,2,1,0:T(8,128)(2,1)S(1)}, u32[]{:S(2)}, u32[]{:S(2)}) %collective-permute-start.17) | collective-permute-done | bytes 589856 | tf_op jit(solution)/shard_map/ppermute | solution.py:28
  87.7 19.6 %collective-permute-done.14 = bf16[2,2,2,32,2048]{4,3,2,1,0:T(8,128)(2,1)S(1)} collective-permute-done((bf16[2,2,2,32,2048]{4,3,2,1,0:T(8,128)(2,1)S(1)}, bf16[2,2,2,32,2048]{4,3,2,1,0:T(8,128)(2,1)S(1)}, u32[]{:S(2)}, u32[]{:S(2)}) %collective-permute-start.14) | collective-permute-done | bytes 1048608 | tf_op jit(solution)/shard_map/ppermute | solution.py:28
  111.4 13.8 %collective-permute-done.22 = bf16[2,144,512]{2,1,0:T(8,128)(2,1)S(1)} collective-permute-done((bf16[2,144,512]{2,1,0:T(8,128)(2,1)S(1)}, bf16[2,144,512]{2,1,0:T(8,128)(2,1)S(1)}, u32[]{:S(2)}, u32[]{:S(2)}) %collective-permute-start.22) | collective-permute-done | bytes 294944 | tf_op jit(solution)/shard_map/ppermute | solution.py:28
  125.4 11.3 %collective-permute-done.19 = bf16[2,2,2,2,32,1152]{5,4,3,2,1,0:T(8,128)(2,1)S(1)} collective-permute-done((bf16[2,2,2,2,32,1152]{5,4,3,2,1,0:T(8,128)(2,1)S(1)}, bf16[2,2,2,2,32,1152]{5,4,3,2,1,0:T(8,128)(2,1)S(1)}, u32[]{:S(2)}, u32[]{:S(2)}) %collective-permute-start.19) | collective-permute-done | bytes 1179680 | tf_op jit(solution)/shard_map/ppermute | solution.py:28
  144.9 4.9 collective-permute-start.25
  158.5 10.3 %collective-permute-done.26 = bf16[256,1024]{1,0:T(8,128)(2,1)S(1)} collective-permute-done((bf16[256,1024]{1,0:T(8,128)(2,1)S(1)}, bf16[256,1024]{1,0:T(8,128)(2,1)S(1)}, u32[]{:S(2)}, u32[]{:S(2)}) %collective-permute-start.26) | collective-permute-done | bytes 524320 | tf_op jit(solution)/shard_map/ppermute | solution.py:28
  171.4 20.4 %collective-permute-done.29 = bf16[512,1024]{1,0:T(8,128)(2,1)S(1)} collective-permute-done((bf16[512,1024]{1,0:T(8,128)(2,1)S(1)}, bf16[512,1024]{1,0:T(8,128)(2,1)S(1)}, u32[]{:S(2)}, u32[]{:S(2)}) %collective-permute-start.29) | collective-permute-done | bytes 1048608 | tf_op jit(solution)/shard_map/ppermute | solution.py:28
  200.8 11.3 %collective-permute-done.28 = bf16[2,2,144,512]{3,2,0,1:T(8,128)(2,1)S(1)} collective-permute-done((bf16[2,2,144,512]{3,2,0,1:T(8,128)(2,1)S(1)}, bf16[2,2,144,512]{3,2,0,1:T(8,128)(2,1)S(1)}, u32[]{:S(2)}, u32[]{:S(2)}) %collective-permute-start.28) | collective-permute-done | bytes 589856 | tf_op jit(solution)/shard_map/ppermute | solution.py:28
  213.6 8.0 %fusion.117 = f32[2048,1152]{1,0:T(8,128)} fusion(bf16[2048,1024]{1,0:T(8,128)(2,1)S(1)} %pad_maximum_fusion.2, bf16[1024,1152]{1,0:T(8,128)(2,1)S(1)} %bitcast.471), kind=kOutput, calls=%fused_computation.335 | convolution fusion | flops 4831838208 | bytes 15990784 | tf_op jit(solution)/shard_map/dot_general | solution.py:112
  221.6 10.4 %multiply_convert_fusion.2 = (bf16[2048,1152]{1,0:T(8,128)(2,1)S(1)}, f32[2048,1152]{1,0:T(8,128)}) fusion(f32[2048,1152]{1,0:T(8,128)} %fusion.117, bf16[2048,1024]{1,0:T(8,128)(2,1)S(1)} %pad_maximum_fusion.2, bf16[1024,1152]{1,0:T(8,128)(2,1)S(1)} %bitcast.476), kind=kOutput, calls=%fused_computation.2 | convolution fusion | flops 4845993984 | bytes 30146560 | tf_op jit(solution)/shard_map/dot_general | solution.py:112
  232.0 5.3 %convolution_convert_fusion.3 = bf16[1152,1024]{1,0:T(8,128)(2,1)S(1)} fusion(bf16[2048,1152]{1,0:T(8,128)(2,1)S(1)} %get-tuple-element.136, bf16[2048,1024]{1,0:T(8,128)(2,1)S(1)} %pad_maximum_fusion.3), kind=kOutput, calls=%fused_computation.20 | convolution fusion | flops 4833017856 | bytes 11272192 | tf_op jit(solution)/shard_map/dot_general | solution.py:116
  239.1 14.4 %multiply_convert_fusion.1 = (bf16[2048,1152]{1,0:T(8,128)(2,1)}, bf16[2048,1152]{1,0:T(8,128)(2,1)}) fusion(f32[2048,1152]{1,0:T(8,128)} %fusion.117, f32[2048,1152]{1,0:T(8,128)} %get-tuple-element.289, bf16[2048,1024]{1,0:T(8,128)(2,1)S(1)} %pad_maximum_fusion.3, bf16[1152,512]{1,0:T(8,128)(2,1)} %bitcast.485, bf16[1152,512]{1,0:T(8,128)(2,1)S(1)} %bitcast.482), kind=kOutput, calls=%fused_computation.1 | convolution fusion | flops 4867227648 | bytes 34865152 | tf_op jit(solution)/shard_map/dot_general | solution.py:122
  253.5 5.4 %fusion.10 = f32[1024,1024]{1,0:T(8,128)S(1)} fusion(bf16[1024,1152]{1,0:T(8,128)(2,1)} %bitcast.477, bf16[2048,1152]{1,0:T(8,128)(2,1)} %get-tuple-element.135), kind=kOutput, calls=%fused_computation.30 | convolution fusion | flops 2415919104 | bytes 8912896 | tf_op jit(solution)/shard_map/dot_general | solution.py:122
  269.4 10.4 %collective-permute-done.32 = bf16[2,2,144,512]{3,2,1,0:T(8,128)(2,1)S(1)} collective-permute-done((bf16[2,2,144,512]{3,2,1,0:T(8,128)(2,1)S(1)}, bf16[2,2,144,512]{3,2,1,0:T(8,128)(2,1)S(1)}, u32[]{:S(2)}, u32[]{:S(2)}) %collective-permute-start.32) | collective-permute-done | bytes 589856 | tf_op jit(solution)/shard_map/ppermute | solution.py:28
  280.0 12.1 %collective-permute-done.33 = bf16[2,2,144,512]{3,2,0,1:T(8,128)(2,1)S(1)} collective-permute-done((bf16[2,2,144,512]{3,2,0,1:T(8,128)(2,1)S(1)}, bf16[2,2,144,512]{3,2,0,1:T(8,128)(2,1)S(1)}, u32[]{:S(2)}, u32[]{:S(2)}) %collective-permute-start.33) | collective-permute-done | bytes 589856 | tf_op jit(solution)/shard_map/ppermute | solution.py:28
  292.3 4.6 convert_add_fusion.3
  300.6 6.1 %convolution_convert_fusion.2 = bf16[1024,1152]{1,0:T(8,128)(2,1)S(1)} fusion(bf16[2048,1024]{1,0:T(8,128)(2,1)S(1)} %copy-done.24, bf16[2048,1152]{1,0:T(8,128)(2,1)S(1)} %bitcast.502), kind=kOutput, calls=%fused_computation.19 | convolution fusion | flops 4833017856 | bytes 11272192 | tf_op jit(solution)/shard_map/dot_general | solution.py:116
  313.1 6.3 %convolution_convert_fusion.1 = bf16[1024,1152]{1,0:T(8,128)(2,1)S(1)} fusion(bf16[2048,1024]{1,0:T(8,128)(2,1)S(1)} %copy-done.24, bf16[2048,1152]{1,0:T(8,128)(2,1)S(1)} %copy-done.67), kind=kOutput, calls=%fused_computation.18 | convolution fusion | flops 4833017856 | bytes 11272192 | tf_op jit(solution)/shard_map/dot_general | solution.py:116
  323.4 9.8 %collective-permute-done.38 = bf16[512,1024]{1,0:T(8,128)(2,1)S(1)} collective-permute-done((bf16[512,1024]{1,0:T(8,128)(2,1)S(1)}, bf16[512,1024]{1,0:T(8,128)(2,1)S(1)}, u32[]{:S(2)}, u32[]{:S(2)}) %collective-permute-start.38) | collective-permute-done | bytes 1048608 | tf_op jit(solution)/shard_map/ppermute | solution.py:28
  363.0 6.9 %copy.82 = bf16[1024,2048]{1,0:T(8,128)(2,1)} copy(bf16[1024,2048]{0,1:T(8,128)(2,1)} %pad_maximum_fusion.4) | data formatting | bytes 8388608 | tf_op jit(solution)/shard_map/concatenate | solution.py:322
  383.2 7.5 %collective-permute-done.43 = bf16[144,512]{1,0:T(8,128)(2,1)S(1)} collective-permute-done((bf16[144,512]{1,0:T(8,128)(2,1)S(1)}, bf16[144,512]{1,0:T(8,128)(2,1)S(1)}, u32[]{:S(2)}, u32[]{:S(2)}) %collective-permute-start.43) | collective-permute-done | bytes 147488 | tf_op jit(solution)/shard_map/ppermute | solution.py:28
  392.0 9.0 %collective-permute-done.45 = bf16[512,1024]{1,0:T(8,128)(2,1)S(1)} collective-permute-done((bf16[512,1024]{1,0:T(8,128)(2,1)S(1)}, bf16[512,1024]{1,0:T(8,128)(2,1)S(1)}, u32[]{:S(2)}, u32[]{:S(2)}) %collective-permute-start.45) | collective-permute-done | bytes 1048608 | tf_op jit(solution)/shard_map/ppermute | solution.py:28
  420.9 6.1 %collective-permute-start.52 = (f32[144,1024]{1,0:T(8,128)}, f32[144,1024]{1,0:T(8,128)}, u32[]{:S(2)}, u32[]{:S(2)}) collective-permute-start(f32[144,1024]{1,0:T(8,128)} %pad_maximum_fusion.27), channel_id=1, source_target_pairs={{0,0},{1,8},{2,16},{3,24},{4,4},{5,12},{6,20},{7,28},{8,1},{9,9},{... | collective-permute-start | bytes 1769480 | tf_op jit(solution)/shard_map/ppermute | solution.py:137
  430.8 14.3 %collective-permute-done.51 = bf16[2,2,32,1152]{3,2,1,0:T(8,128)(2,1)} collective-permute-done((bf16[2,2,32,1152]{3,2,1,0:T(8,128)(2,1)S(1)}, bf16[2,2,32,1152]{3,2,1,0:T(8,128)(2,1)}, u32[]{:S(2)}, u32[]{:S(2)}) %collective-permute-start.51) | collective-permute-done | bytes 294944 | tf_op jit(solution)/shard_map/ppermute | solution.py:28
  464.9 4.5 collective-permute-done.56
  469.6 4.5 collective-permute-done.57
  484.7 10.1 %collective-permute-done.61 = bf16[2,32,2048]{2,1,0:T(8,128)(2,1)S(1)} collective-permute-done((bf16[2,32,2048]{2,1,0:T(8,128)(2,1)S(1)}, bf16[2,32,2048]{2,1,0:T(8,128)(2,1)S(1)}, u32[]{:S(2)}, u32[]{:S(2)}) %collective-permute-start.61) | collective-permute-done | bytes 262176 | tf_op jit(solution)/shard_map/ppermute | solution.py:28
  (446 shorter events, 209.6 us)
Async XLA Ops:
  39.3 17.3 %collective-permute-start.10 = (bf16[2,2,32,2048]{3,2,1,0:T(8,128)(2,1)S(1)}, bf16[2,2,32,2048]{3,2,1,0:T(8,128)(2,1)S(1)}, u32[]{:S(2)}, u32[]{:S(2)}) collective-permute-start(bf16[2,2,32,2048]{3,2,1,0:T(8,128)(2,1)S(1)} %pad_maximum_fusion.31), channel_id=1, source_target_pairs={{0,4},{2,6},{4,0},{6,2},{8,12},{10,14},{12,8},{14,10},{16,20},{18,... | collective-permute-start | bytes 1572872 | tf_op jit(solution)/shard_map/ppermute | solution.py:28
  39.8 17.0 %collective-permute-start.11 = (bf16[2,2,32,2176]{3,2,1,0:T(8,128)(2,1)S(1)}, bf16[2,2,32,2176]{3,2,1,0:T(8,128)(2,1)S(1)}, u32[]{:S(2)}, u32[]{:S(2)}) collective-permute-start(bf16[2,2,32,2176]{3,2,1,0:T(8,128)(2,1)S(1)} %pad_maximum_fusion.30), channel_id=1, source_target_pairs={{0,1},{1,0},{2,3},{3,2},{4,5},{5,4},{6,7},{7,6},{8,9},{9,8},{10,11... | collective-permute-start | bytes 1671176 | tf_op jit(solution)/shard_map/ppermute | solution.py:28
  57.0 21.8 %collective-permute-start.16 = (bf16[2,2,2,32,1152]{4,3,2,1,0:T(8,128)(2,1)S(1)}, bf16[2,2,2,32,1152]{4,3,2,1,0:T(8,128)(2,1)S(1)}, u32[]{:S(2)}, u32[]{:S(2)}) collective-permute-start(bf16[2,2,2,32,1152]{4,3,2,1,0:T(8,128)(2,1)S(1)} %pad_maximum_fusion.23), channel_id=1, source_target_pairs={{0,16},{2,18},{4,20},{6,22},{8,24},{10,26},{12,28},{14,30},{16,0},... | collective-permute-start | bytes 1769480 | tf_op jit(solution)/shard_map/ppermute | solution.py:28
  57.1 30.2 %collective-permute-start.17 = (bf16[2,2,2,32,1152]{4,3,2,1,0:T(8,128)(2,1)S(1)}, bf16[2,2,2,32,1152]{4,3,2,1,0:T(8,128)(2,1)S(1)}, u32[]{:S(2)}, u32[]{:S(2)}) collective-permute-start(bf16[2,2,2,32,1152]{4,3,2,1,0:T(8,128)(2,1)S(1)} %pad_maximum_fusion.24), channel_id=1, source_target_pairs={{0,8},{2,10},{4,12},{6,14},{8,0},{10,2},{12,4},{14,6},{16,24},{18,... | collective-permute-start | bytes 1769480 | tf_op jit(solution)/shard_map/ppermute | solution.py:28
  69.0 39.4 %collective-permute-start.20 = (bf16[2,144,1024]{2,1,0:T(8,128)(2,1)S(1)}, bf16[2,144,1024]{2,1,0:T(8,128)(2,1)S(1)}, u32[]{:S(2)}, u32[]{:S(2)}) collective-permute-start(bf16[2,144,1024]{2,1,0:T(8,128)(2,1)S(1)} %pad_maximum_fusion.22), channel_id=1, source_target_pairs={{0,0},{1,8},{2,16},{3,24},{4,4},{5,12},{6,20},{7,28},{8,1},{9,9},{... | collective-permute-start | bytes 1769480 | tf_op jit(solution)/shard_map/ppermute | solution.py:137
  69.7 37.6 %collective-permute-start.14 = (bf16[2,2,2,32,2048]{4,3,2,1,0:T(8,128)(2,1)S(1)}, bf16[2,2,2,32,2048]{4,3,2,1,0:T(8,128)(2,1)S(1)}, u32[]{:S(2)}, u32[]{:S(2)}) collective-permute-start(bf16[2,2,2,32,2048]{4,3,2,1,0:T(8,128)(2,1)S(1)} %pad_maximum_fusion.18), channel_id=1, source_target_pairs={{0,1},{1,0},{2,3},{3,2},{4,5},{5,4},{6,7},{7,6},{8,9},{9,8},{10,11... | collective-permute-start | bytes 3145736 | tf_op jit(solution)/shard_map/ppermute | solution.py:28
  72.4 35.4 %collective-permute-start.15 = (bf16[2,2,2,32,2176]{4,3,2,1,0:T(8,128)(2,1)S(1)}, bf16[2,2,2,32,2176]{4,3,2,1,0:T(8,128)(2,1)S(1)}, u32[]{:S(2)}, u32[]{:S(2)}) collective-permute-start(bf16[2,2,2,32,2176]{4,3,2,1,0:T(8,128)(2,1)S(1)} %pad_maximum_fusion.17), channel_id=1, source_target_pairs={{0,4},{2,6},{4,0},{6,2},{8,12},{10,14},{12,8},{14,10},{16,20},{18,... | collective-permute-start | bytes 3342344 | tf_op jit(solution)/shard_map/ppermute | solution.py:28
  108.3 28.7 %collective-permute-start.24 = (bf16[2,2,2,2,32,2048]{5,4,3,2,1,0:T(8,128)(2,1)S(1)}, bf16[2,2,2,2,32,2048]{5,4,3,2,1,0:T(8,128)(2,1)S(1)}, u32[]{:S(2)}, u32[]{:S(2)}) collective-permute-start(bf16[2,2,2,2,32,2048]{5,4,3,2,1,0:T(8,128)(2,1)S(1)} %pad_maximum_fusion.9), channel_id=1, source_target_pairs={{0,2},{2,0},{4,6},{6,4},{8,10},{10,8},{12,14},{14,12},{16,18},{18,... | collective-permute-start | bytes 6291464 | tf_op jit(solution)/shard_map/ppermute | solution.py:28
  108.4 28.4 %collective-permute-start.19 = (bf16[2,2,2,2,32,1152]{5,4,3,2,1,0:T(8,128)(2,1)S(1)}, bf16[2,2,2,2,32,1152]{5,4,3,2,1,0:T(8,128)(2,1)S(1)}, u32[]{:S(2)}, u32[]{:S(2)}) collective-permute-start(bf16[2,2,2,2,32,1152]{5,4,3,2,1,0:T(8,128)(2,1)S(1)} %pad_maximum_fusion.13), channel_id=1, source_target_pairs={{0,4},{2,6},{4,0},{6,2},{8,12},{10,14},{12,8},{14,10},{16,20},{18,... | collective-permute-start | bytes 3538952 | tf_op jit(solution)/shard_map/ppermute | solution.py:28
  111.2 26.8 %collective-permute-start.23 = (bf16[2,2,2,2,32,2176]{5,4,3,2,1,0:T(8,128)(2,1)S(1)}, bf16[2,2,2,2,32,2176]{5,4,3,2,1,0:T(8,128)(2,1)S(1)}, u32[]{:S(2)}, u32[]{:S(2)}) collective-permute-start(bf16[2,2,2,2,32,2176]{5,4,3,2,1,0:T(8,128)(2,1)S(1)} %pad_maximum_fusion.8), channel_id=1, source_target_pairs={{0,2},{2,0},{4,6},{6,4},{8,10},{10,8},{12,14},{14,12},{16,18},{18,... | collective-permute-start | bytes 6684680 | tf_op jit(solution)/shard_map/ppermute | solution.py:28
  168.8 22.9 %collective-permute-start.29 = (bf16[512,1024]{1,0:T(8,128)(2,1)S(1)}, bf16[512,1024]{1,0:T(8,128)(2,1)S(1)}, u32[]{:S(2)}, u32[]{:S(2)}) collective-permute-start(bf16[512,1024]{1,0:T(8,128)(2,1)S(1)} %multiply_convert_fusion.5), channel_id=1, source_target_pairs={{0,1},{1,0},{2,3},{3,2},{4,5},{5,4},{6,7},{7,6},{8,9},{9,8},{10,11... | collective-permute-start | bytes 3145736 | tf_op jit(solution)/shard_map/ppermute | solution.py:28
  170.6 25.2 %collective-permute-start.18 = (bf16[2,2,2,2,32,1152]{5,4,3,2,0,1:T(8,128)(2,1)S(1)}, bf16[2,2,2,2,32,1152]{5,4,3,2,0,1:T(8,128)(2,1)S(1)}, u32[]{:S(2)}, u32[]{:S(2)}) collective-permute-start(bf16[2,2,2,2,32,1152]{5,4,3,2,0,1:T(8,128)(2,1)S(1)} %pad_maximum_fusion.14), channel_id=1, source_target_pairs={{0,4},{2,6},{4,0},{6,2},{8,12},{10,14},{12,8},{14,10},{16,20},{18,... | collective-permute-start | bytes 3538952 | tf_op jit(solution)/shard_map/ppermute | solution.py:28
  171.2 41.1 %collective-permute-start.31 = (bf16[1024,1024]{1,0:T(8,128)(2,1)S(1)}, bf16[1024,1024]{1,0:T(8,128)(2,1)S(1)}, u32[]{:S(2)}, u32[]{:S(2)}) collective-permute-start(bf16[1024,1024]{1,0:T(8,128)(2,1)S(1)} %pad_maximum_fusion.11), channel_id=1, source_target_pairs={{0,2},{2,0},{4,6},{6,4},{8,10},{10,8},{12,14},{14,12},{16,18},{18,... | collective-permute-start | bytes 6291464 | tf_op jit(solution)/shard_map/ppermute | solution.py:28
  171.3 28.2 %collective-permute-start.27 = (bf16[2,2,144,512]{3,2,1,0:T(8,128)(2,1)S(1)}, bf16[2,2,144,512]{3,2,1,0:T(8,128)(2,1)S(1)}, u32[]{:S(2)}, u32[]{:S(2)}) collective-permute-start(bf16[2,2,144,512]{3,2,1,0:T(8,128)(2,1)S(1)} %pad_maximum_fusion.25), channel_id=1, source_target_pairs={{0,16},{2,18},{4,20},{6,22},{8,24},{10,26},{12,28},{14,30},{16,0},... | collective-permute-start | bytes 1769480 | tf_op jit(solution)/shard_map/ppermute | solution.py:28
  191.9 20.9 %collective-permute-start.30 = (bf16[1024,1024]{1,0:T(8,128)(2,1)S(1)}, bf16[1024,1024]{1,0:T(8,128)(2,1)S(1)}, u32[]{:S(2)}, u32[]{:S(2)}) collective-permute-start(bf16[1024,1024]{1,0:T(8,128)(2,1)S(1)} %pad_maximum_fusion.10), channel_id=1, source_target_pairs={{0,2},{2,0},{4,6},{6,4},{8,10},{10,8},{12,14},{14,12},{16,18},{18,... | collective-permute-start | bytes 6291464 | tf_op jit(solution)/shard_map/ppermute | solution.py:28
  263.2 29.0 %collective-permute-start.34 = (bf16[1024,1024]{1,0:T(8,128)(2,1)}, bf16[1024,1024]{1,0:T(8,128)(2,1)}, u32[]{:S(2)}, u32[]{:S(2)}) collective-permute-start(bf16[1024,1024]{1,0:T(8,128)(2,1)} %add_convert_fusion), channel_id=1, source_target_pairs={{0,2},{2,0},{4,6},{6,4},{8,10},{10,8},{12,14},{14,12},{16,18},{18,... | collective-permute-start | bytes 6291464 | tf_op jit(solution)/shard_map/ppermute | solution.py:28
  265.5 26.6 %collective-permute-start.33 = (bf16[2,2,144,512]{3,2,0,1:T(8,128)(2,1)S(1)}, bf16[2,2,144,512]{3,2,0,1:T(8,128)(2,1)S(1)}, u32[]{:S(2)}, u32[]{:S(2)}) collective-permute-start(bf16[2,2,144,512]{3,2,0,1:T(8,128)(2,1)S(1)} %dynamic-slice_bitcast_fusion.7), channel_id=1, source_target_pairs={{0,4},{2,6},{4,0},{6,2},{8,12},{10,14},{12,8},{14,10},{16,20},{18,... | collective-permute-start | bytes 1769480 | tf_op jit(solution)/shard_map/ppermute | solution.py:28
  306.8 27.7 %collective-permute-start.35 = (bf16[2,2,2,2,32,1152]{5,4,3,2,1,0:T(8,128)(2,1)S(1)}, bf16[2,2,2,2,32,1152]{5,4,3,2,1,0:T(8,128)(2,1)S(1)}, u32[]{:S(2)}, u32[]{:S(2)}) collective-permute-start(bf16[2,2,2,2,32,1152]{5,4,3,2,1,0:T(8,128)(2,1)S(1)} %dynamic-slice_bitcast_fusion.2), channel_id=1, source_target_pairs={{0,4},{2,6},{4,0},{6,2},{8,12},{10,14},{12,8},{14,10},{16,20},{18,... | collective-permute-start | bytes 3538952 | tf_op jit(solution)/shard_map/ppermute | solution.py:28
  308.8 24.5 %collective-permute-start.38 = (bf16[512,1024]{1,0:T(8,128)(2,1)S(1)}, bf16[512,1024]{1,0:T(8,128)(2,1)S(1)}, u32[]{:S(2)}, u32[]{:S(2)}) collective-permute-start(bf16[512,1024]{1,0:T(8,128)(2,1)S(1)} %slice.386), channel_id=1, source_target_pairs={{0,1},{1,0},{2,3},{3,2},{4,5},{5,4},{6,7},{7,6},{8,9},{9,8},{10,11... | collective-permute-start | bytes 3145736 | tf_op jit(solution)/shard_map/ppermute | solution.py:28
  313.0 21.8 %collective-permute-start.39 = (bf16[1024,1024]{1,0:T(8,128)(2,1)S(1)}, bf16[1024,1024]{1,0:T(8,128)(2,1)S(1)}, u32[]{:S(2)}, u32[]{:S(2)}) collective-permute-start(bf16[1024,1024]{1,0:T(8,128)(2,1)S(1)} %fusion.41), channel_id=1, source_target_pairs={{0,2},{2,0},{4,6},{6,4},{8,10},{10,8},{12,14},{14,12},{16,18},{18,... | collective-permute-start | bytes 6291464 | tf_op jit(solution)/shard_map/ppermute | solution.py:28
  342.0 60.7 %collective-permute-start.40 = (bf16[2,2,2,2,32,1152]{5,4,3,2,1,0:T(8,128)(2,1)}, bf16[2,2,2,2,32,1152]{5,4,3,2,1,0:T(8,128)(2,1)}, u32[]{:S(2)}, u32[]{:S(2)}) collective-permute-start(bf16[2,2,2,2,32,1152]{5,4,3,2,1,0:T(8,128)(2,1)} %dynamic-slice_bitcast_fusion.1), channel_id=1, source_target_pairs={{0,4},{2,6},{4,0},{6,2},{8,12},{10,14},{12,8},{14,10},{16,20},{18,... | collective-permute-start | bytes 3538952 | tf_op jit(solution)/shard_map/ppermute | solution.py:28
  344.4 46.3 %collective-permute-start.41 = (bf16[2,2,2,32,1152]{4,3,2,1,0:T(8,128)(2,1)}, bf16[2,2,2,32,1152]{4,3,2,1,0:T(8,128)(2,1)}, u32[]{:S(2)}, u32[]{:S(2)}) collective-permute-start(bf16[2,2,2,32,1152]{4,3,2,1,0:T(8,128)(2,1)} %dynamic-slice_bitcast_fusion.6), channel_id=1, source_target_pairs={{0,16},{2,18},{4,20},{6,22},{8,24},{10,26},{12,28},{14,30},{16,0},... | collective-permute-start | bytes 1769480 | tf_op jit(solution)/shard_map/ppermute | solution.py:28
  345.8 35.7 %collective-permute-start.42 = (bf16[144,512]{1,0:T(8,128)(2,1)}, bf16[144,512]{1,0:T(8,128)(2,1)}, u32[]{:S(2)}, u32[]{:S(2)}) collective-permute-start(bf16[144,512]{1,0:T(8,128)(2,1)} %dynamic-slice_bitcast_fusion.20), channel_id=1, source_target_pairs={{0,8},{2,10},{4,12},{6,14},{8,0},{10,2},{12,4},{14,6},{16,24},{18,... | collective-permute-start | bytes 442376 | tf_op jit(solution)/shard_map/ppermute | solution.py:28
  372.0 32.3 %collective-permute-start.47 = (bf16[2,2,2,2,32,2048]{5,4,3,2,1,0:T(8,128)(2,1)S(1)}, bf16[2,2,2,2,32,2048]{5,4,3,2,1,0:T(8,128)(2,1)S(1)}, u32[]{:S(2)}, u32[]{:S(2)}) collective-permute-start(bf16[2,2,2,2,32,2048]{5,4,3,2,1,0:T(8,128)(2,1)S(1)} %dynamic-slice_bitcast_fusion), channel_id=1, source_target_pairs={{0,2},{2,0},{4,6},{6,4},{8,10},{10,8},{12,14},{14,12},{16,18},{18,... | collective-permute-start | bytes 6291464 | tf_op jit(solution)/shard_map/ppermute | solution.py:28
  375.2 25.8 %collective-permute-start.45 = (bf16[512,1024]{1,0:T(8,128)(2,1)S(1)}, bf16[512,1024]{1,0:T(8,128)(2,1)S(1)}, u32[]{:S(2)}, u32[]{:S(2)}) collective-permute-start(bf16[512,1024]{1,0:T(8,128)(2,1)S(1)} %copy-done.44), channel_id=1, source_target_pairs={{0,1},{1,0},{2,3},{3,2},{4,5},{5,4},{6,7},{7,6},{8,9},{9,8},{10,11... | collective-permute-start | bytes 3145736 | tf_op jit(solution)/shard_map/ppermute | solution.py:28
  407.0 42.2 %collective-permute-start.48 = (bf16[2,2,2,32,2048]{4,3,1,0,2:T(8,128)(2,1)}, bf16[2,2,2,32,2048]{4,3,1,0,2:T(8,128)(2,1)}, u32[]{:S(2)}, u32[]{:S(2)}) collective-permute-start(bf16[2,2,2,32,2048]{4,3,1,0,2:T(8,128)(2,1)} %dynamic-slice_bitcast_fusion.4), channel_id=1, source_target_pairs={{0,1},{1,0},{2,3},{3,2},{4,5},{5,4},{6,7},{7,6},{8,9},{9,8},{10,11... | collective-permute-start | bytes 3145736 | tf_op jit(solution)/shard_map/ppermute | solution.py:28
  409.8 41.0 %collective-permute-start.49 = (bf16[2,2,2,32,2048]{4,3,2,1,0:T(8,128)(2,1)}, bf16[2,2,2,32,2048]{4,3,2,1,0:T(8,128)(2,1)}, u32[]{:S(2)}, u32[]{:S(2)}) collective-permute-start(bf16[2,2,2,32,2048]{4,3,2,1,0:T(8,128)(2,1)} %dynamic-slice_bitcast_fusion.3), channel_id=1, source_target_pairs={{0,4},{2,6},{4,0},{6,2},{8,12},{10,14},{12,8},{14,10},{16,20},{18,... | collective-permute-start | bytes 3145736 | tf_op jit(solution)/shard_map/ppermute | solution.py:28
  412.3 34.7 %collective-permute-start.50 = (bf16[2,2,2,32,1152]{4,3,2,1,0:T(8,128)(2,1)}, bf16[2,2,2,32,1152]{4,3,2,1,0:T(8,128)(2,1)}, u32[]{:S(2)}, u32[]{:S(2)}) collective-permute-start(bf16[2,2,2,32,1152]{4,3,2,1,0:T(8,128)(2,1)} %dynamic-slice_bitcast_fusion.5), channel_id=1, source_target_pairs={{0,8},{2,10},{4,12},{6,14},{8,0},{10,2},{12,4},{14,6},{16,24},{18,... | collective-permute-start | bytes 1769480 | tf_op jit(solution)/shard_map/ppermute | solution.py:28
  412.7 32.5 %collective-permute-start.51 = (bf16[2,2,32,1152]{3,2,1,0:T(8,128)(2,1)S(1)}, bf16[2,2,32,1152]{3,2,1,0:T(8,128)(2,1)}, u32[]{:S(2)}, u32[]{:S(2)}) collective-permute-start(bf16[2,2,32,1152]{3,2,1,0:T(8,128)(2,1)S(1)} %dynamic-slice_bitcast_fusion.14), channel_id=1, source_target_pairs={{0,8},{2,10},{4,12},{6,14},{8,0},{10,2},{12,4},{14,6},{16,24},{18,... | collective-permute-start | bytes 884744 | tf_op jit(solution)/shard_map/ppermute | solution.py:28
  420.9 32.5 %collective-permute-start.52 = (f32[144,1024]{1,0:T(8,128)}, f32[144,1024]{1,0:T(8,128)}, u32[]{:S(2)}, u32[]{:S(2)}) collective-permute-start(f32[144,1024]{1,0:T(8,128)} %pad_maximum_fusion.27), channel_id=1, source_target_pairs={{0,0},{1,8},{2,16},{3,24},{4,4},{5,12},{6,20},{7,28},{8,1},{9,9},{... | collective-permute-start | bytes 1769480 | tf_op jit(solution)/shard_map/ppermute | solution.py:137
  454.7 26.8 %collective-permute-start.58 = (bf16[2,2,32,2048]{3,2,1,0:T(8,128)(2,1)S(1)}, bf16[2,2,32,2048]{3,2,1,0:T(8,128)(2,1)S(1)}, u32[]{:S(2)}, u32[]{:S(2)}) collective-permute-start(bf16[2,2,32,2048]{3,2,1,0:T(8,128)(2,1)S(1)} %dynamic-slice_bitcast_fusion.10), channel_id=1, source_target_pairs={{0,4},{2,6},{4,0},{6,2},{8,12},{10,14},{12,8},{14,10},{16,20},{18,... | collective-permute-start | bytes 1572872 | tf_op jit(solution)/shard_map/ppermute | solution.py:28
  459.8 21.9 %collective-permute-start.59 = (bf16[2,2,32,2048]{3,2,1,0:T(8,128)(2,1)S(1)}, bf16[2,2,32,2048]{3,2,1,0:T(8,128)(2,1)S(1)}, u32[]{:S(2)}, u32[]{:S(2)}) collective-permute-start(bf16[2,2,32,2048]{3,2,1,0:T(8,128)(2,1)S(1)} %dynamic-slice_bitcast_fusion.9), channel_id=1, source_target_pairs={{0,1},{1,0},{2,3},{3,2},{4,5},{5,4},{6,7},{7,6},{8,9},{9,8},{10,11... | collective-permute-start | bytes 1572872 | tf_op jit(solution)/shard_map/ppermute | solution.py:28
  (112 other events, 1085.3 us)

commit v3 on v2

v3 whole, which is shorter than its diff:
```python
import jax
import jax.numpy as jnp
from jax import lax
from jax.sharding import PartitionSpec as P

EPSILON = 1e-05
CORE = ("fsdp", 0)
SIDE = ("seq", 0)


def shifted(shard, axis, by):
    size = lax.axis_size(axis)
    pairs = [(i, i + by) for i in range(size) if 0 <= i + by < size]
    return lax.ppermute(shard, axis, pairs)


def bit_count(axis):
    return lax.axis_size(axis).bit_length() - 1


def my_bit(dim):
    axis, bit = dim
    return (lax.axis_index(axis) >> bit) & 1


def swap(value, dim):
    axis, bit = dim
    return lax.ppermute(value, axis, [(i, i ^ (1 << bit)) for i in range(lax.axis_size(axis))])


def rank(dim):
    axis, bit = dim
    return (0 if axis == "fsdp" else 1, -bit)


def down_rank(dim):
    top = bit_count("fsdp") - 1
    return rank({("fsdp", top): CORE, ("fsdp", top - 1): SIDE}.get(dim, dim))


def tie(*values):
    return lax.optimization_barrier(values)


class Chain:
    def __init__(self, buffer, dims, held, order):
        self.buffer, self.left, self.held, self.order = buffer, list(dims), list(held), order
        self.parts = []

    def start(self):
        if self.left:
            self.parts = [swap(self.sent(), self.left[0])]

    def start_half(self, half):
        if self.left:
            sent = self.sent()
            middle = sent.shape[0] // 2
            part = swap(sent[middle:] if half else sent[:middle], self.left[0])
            self.parts = self.parts + [part] if half else [part]

    def merge(self):
        if self.left:
            other = self.parts[0] if len(self.parts) == 1 else jnp.concatenate(self.parts, axis=0)
            self.parts = []
            self.take(self.left.pop(0), other)


class Gather(Chain):
    def __init__(self, piece, dims, held=(), order=rank):
        super().__init__(piece, dims, held, order)

    def sent(self):
        return self.buffer

    def take(self, dim, other):
        axis = sum(self.order(h) < self.order(dim) for h in self.held)
        high = my_bit(dim) == 1
        self.buffer = jnp.stack(
            [jnp.where(high, other, self.buffer), jnp.where(high, self.buffer, other)], axis=axis
        )
        self.held.append(dim)


class Scatter(Chain):
    def __init__(self, terms, dims, held, order=rank):
        super().__init__(terms, dims, sorted(held, key=order), order)

    def sent(self):
        axis, bit = self.held.index(self.left[0]), my_bit(self.left[0])
        return lax.dynamic_index_in_dim(self.buffer, 1 - bit, axis, keepdims=False)

    def take(self, dim, other):
        axis, bit = self.held.index(dim), my_bit(dim)
        keep = lax.dynamic_index_in_dim(self.buffer, bit, axis, keepdims=False)
        total = keep.astype(jnp.float32) + other.astype(jnp.float32)
        self.buffer = total.astype(jnp.bfloat16) if self.left else total
        self.held.remove(dim)


def tie_chains(chains, *others, parts=True):
    count = [len(chain.parts) if parts else 0 for chain in chains]
    flat = [p for chain, n in zip(chains, count) for p in chain.parts[:n]]
    tied = list(tie(*(chain.buffer for chain in chains), *flat, *others))
    for chain in chains:
        chain.buffer = tied.pop(0)
    for chain, n in zip(chains, count):
        chain.parts = [tied.pop(0) for _ in range(n)] + chain.parts[n:]
    return tied


def advance(chains, *others, first=(), second=()):
    for chain in chains:
        chain.start()
    for chain in first:
        chain.start_half(0)
    for chain in second:
        chain.start_half(1)
    every = [*chains, *first, *second]
    others = tie_chains(every, *others, parts=False)
    for chain in [*chains, *second]:
        chain.merge()
    return tie_chains(every, *others)


def step(chain):
    chain.start()
    chain.merge()


def finish(*chains):
    for chain in chains:
        while chain.left:
            step(chain)


def normalize(values, gain):
    scale = lax.rsqrt(jnp.mean(values * values, axis=-1, keepdims=True) + EPSILON)
    normalized_rows = values * scale
    return (normalized_rows, scale, normalized_rows * gain)


def norm_back(d_hidden, normalized_rows, scale, gain):
    norm_gradient = d_hidden * gain
    grad_gain = jnp.sum(d_hidden * normalized_rows, axis=0)
    d_input = scale * (
        norm_gradient
        - normalized_rows * jnp.mean(norm_gradient * normalized_rows, axis=-1, keepdims=True)
    )
    return (d_input, grad_gain)


def dot_plain(left_segment, right_segment):
    return jnp.dot(left_segment, right_segment, preferred_element_type=jnp.float32)


def dot_first(left_segment, right_segment):
    return lax.dot_general(
        left_segment, right_segment, (((0,), (0,)), ((), ())), preferred_element_type=jnp.float32
    )


def dot_second(left_segment, right_segment):
    return lax.dot_general(
        left_segment, right_segment, (((1,), (1,)), ((), ())), preferred_element_type=jnp.float32
    )


def quarter_owner_swap(value):
    fsdp, seq = lax.axis_size("fsdp"), lax.axis_size("seq")
    top = bit_count("fsdp") - 1
    pairs = []
    for device in range(fsdp * seq):
        f, s = divmod(device, seq)
        high, low = (f >> top) & 1, (f >> (top - 1)) & 1
        core, side = f & 1, s & 1
        f2 = (f & ~((1 << top) | (1 << (top - 1)) | 1)) | (core << top) | (side << (top - 1)) | high
        pairs.append((device, f2 * seq + ((s & ~1) | low)))
    return lax.ppermute(value, ("fsdp", "seq"), pairs)


def body(tokens, gain_a, mix_in, conv_tap, mix_out, gain_b, ff_gate, ff_up, ff_down, cotangent):
    seq_count, local_rows, feature_width = tokens.shape
    row_total = seq_count * local_rows
    tap_count = conv_tap.shape[0]
    own_rows = mix_in.shape[0]
    hidden_units = ff_gate.shape[1]
    quarter = hidden_units // 4
    core, side = my_bit(CORE), my_bit(SIDE)
    near = [("fsdp", 1)]
    far = [("fsdp", b) for b in range(2, bit_count("fsdp"))]
    outer = [("seq", b) for b in range(1, bit_count("seq"))]
    zx, zx_turned = far + near + outer, far[::-1] + near + outer
    route_a, route_b = far + near + outer + [SIDE], far[::-1] + [SIDE] + outer + near
    group = [CORE, SIDE]
    half_width = 2 * feature_width
    down_half = feature_width // 2

    def ordered(pair_bit, mine, other):
        high = pair_bit == 1
        return jnp.where(high, other, mine), jnp.where(high, mine, other)

    small = jnp.concatenate([gain_a[None], gain_b[None], conv_tap], axis=0).T
    small = jnp.pad(small, ((0, 0), (0, 128 - small.shape[1])))
    mix_a = Gather(
        jnp.concatenate([mix_in[:, :feature_width], mix_in[:, 2 * feature_width :]], axis=1), route_a
    )
    mix_b = Gather(
        jnp.concatenate([mix_in[:, feature_width : 2 * feature_width], mix_out, small], axis=1),
        route_b,
    )
    down_piece = quarter_owner_swap(ff_down)

    def quarters(shard):
        return jnp.stack([shard[:, q * quarter : (q + 1) * quarter] for q in range(4)]).reshape(
            2, 2, own_rows, quarter
        )

    def regroup(parts, axis, bit, dim):
        mine = lax.dynamic_index_in_dim(parts, bit, axis, keepdims=False)
        other = swap(lax.dynamic_index_in_dim(parts, 1 - bit, axis, keepdims=False), dim)
        return mine, other

    gate_mine, gate_other = regroup(quarters(ff_gate), 1, side, SIDE)
    up_mine, up_other = regroup(quarters(ff_up), 1, side, SIDE)
    cot_low = cotangent.reshape(row_total, feature_width)
    cot_first, cot_last = cot_low[: row_total // 2], cot_low[row_total // 2 :]
    gate_mine, gate_other, up_mine, up_other, cot_first, down_piece = advance(
        [mix_a, mix_b], gate_mine, gate_other, up_mine, up_other, cot_first, down_piece
    )
    down_x = Gather(down_piece, near + outer, (), down_rank)

    def regroup_core(mine, other):
        both = jnp.stack(ordered(side, mine, other), axis=1)
        return jnp.stack(ordered(core, *regroup(both, 0, core, CORE)), axis=0)

    gate = Gather(regroup_core(gate_mine, gate_other), zx_turned, group)
    up = Gather(regroup_core(up_mine, up_other), zx, group)
    cot_first_other = swap(cot_first, SIDE)
    gate.buffer, up.buffer, cot_first_other, cot_last = advance(
        [mix_a, mix_b, down_x], gate.buffer, up.buffer, cot_first_other, cot_last
    )

    finish(down_x)
    while mix_a.left or mix_b.left:
        down_x.buffer, cot_last = advance([mix_a, mix_b, gate, up], down_x.buffer, cot_last)

    inputs = tokens.reshape(row_total, feature_width).astype(jnp.float32)
    cot_full = cot_low.astype(jnp.float32)
    cot_last_other = swap(cot_last, SIDE)
    core_a, core_b = Gather(mix_a.buffer, [CORE], mix_a.held), Gather(mix_b.buffer, [CORE], mix_b.held)
    step(core_a)
    step(core_b)
    weight_bv = core_a.buffer.reshape(feature_width, half_width)
    weight_c_out = core_b.buffer.reshape(feature_width, half_width + 128)
    weight_c = weight_c_out[:, :feature_width]
    weight_out = weight_c_out[:, feature_width:half_width]
    small_whole = weight_c_out[:, half_width : half_width + 2 + tap_count].T.astype(jnp.float32)
    gain_one, gain_two, tap_values = small_whole[0], small_whole[1], small_whole[2:]
    normed_a, scale_a, hidden = normalize(inputs, gain_one)
    hidden_low = hidden.astype(jnp.bfloat16)
    bv_part = dot_plain(hidden_low, weight_bv)
    b_part = bv_part[:, :feature_width]
    v_part = bv_part[:, feature_width:]
    mixed = (b_part * v_part).astype(jnp.bfloat16).reshape(seq_count, local_rows, feature_width)
    mixed, hidden_low, weight_c, down_piece, cot_last_other = advance(
        [], mixed, hidden_low, weight_c, down_x.buffer, cot_last_other, first=[gate]
    )
    edge_rows = shifted(mixed[:, local_rows - (tap_count - 1) :, :], "seq", 1)
    c_part = dot_plain(hidden_low, weight_c)
    extended = jnp.concatenate([edge_rows, mixed], axis=1).astype(jnp.float32)
    convolved = tap_values[0] * extended[:, 0:local_rows]
    for offset in range(1, tap_count):
        convolved = convolved + tap_values[offset] * extended[:, offset : offset + local_rows]
    convolved = convolved.reshape(row_total, feature_width)
    gated = (c_part * convolved).astype(jnp.bfloat16)
    after_mix = inputs + dot_plain(gated, weight_out)
    normed_b, scale_b, hidden_b = normalize(after_mix, gain_two)
    hidden_b_low = hidden_b.astype(jnp.bfloat16)
    down_a = Gather(down_piece[..., :down_half], far, near + outer, down_rank)
    down_b = Gather(down_piece[..., down_half:], far[::-1], near + outer, down_rank)
    (hidden_b_low,) = advance([down_a, down_b], hidden_b_low, first=[up], second=[gate])
    finish(gate)
    weight_gate = gate.buffer.reshape(feature_width, quarter)

    def both_cores(value):
        return jnp.concatenate([value, swap(value, CORE)], axis=0)

    def forward(hidden_rows):
        gate_value = dot_plain(hidden_rows, weight_gate)
        up_value = dot_plain(hidden_rows, weight_up)
        sigmoid_gate = jax.nn.sigmoid(gate_value)
        silu_gate = gate_value * sigmoid_gate
        slope = up_value * (sigmoid_gate * (1.0 + gate_value * (1.0 - sigmoid_gate)))
        active = (silu_gate * up_value).astype(jnp.bfloat16)
        return active, silu_gate.astype(jnp.bfloat16), slope.astype(jnp.bfloat16)

    half_rows = row_total // 2
    hidden_side = [swap(hidden_b_low[:half_rows], SIDE)]
    hidden_near = both_cores(hidden_b_low)
    cot_near = both_cores(cot_low)
    cot_far = both_cores(jnp.concatenate([cot_first_other, cot_last_other], axis=0))
    hidden_near, cot_near, cot_far, hidden_b_low, *hidden_side = advance(
        [], hidden_near, cot_near, cot_far, hidden_b_low, *hidden_side,
        first=[down_a, down_b], second=[up],
    )
    finish(up)
    weight_up = up.buffer.reshape(feature_width, quarter)
    hidden_side.append(swap(hidden_b_low[half_rows:], SIDE))
    active_near, silu_near, slope_near = forward(hidden_near)
    grad_down_near = dot_first(active_near, cot_near)
    active_near, silu_near, slope_near, grad_down_near, *hidden_side = advance(
        [], active_near, silu_near, slope_near, grad_down_near, *hidden_side,
        second=[down_a, down_b],
    )
    finish(down_a, down_b)
    weight_down = jnp.concatenate(
        [down_a.buffer.reshape(quarter, down_half), down_b.buffer.reshape(quarter, down_half)], axis=1
    )

    hidden_far = both_cores(jnp.concatenate(hidden_side, axis=0))
    active_far, silu_far, slope_far = forward(hidden_far)

    def split(gradient, rows):
        return gradient.astype(jnp.bfloat16).reshape((2,) * len(zx) + rows)

    grad_down = split(grad_down_near + dot_first(active_far, cot_far), (-1, feature_width))
    grad_down, hidden_far, active_far, silu_far, slope_far = tie(
        grad_down, hidden_far, active_far, silu_far, slope_far
    )
    grad_down_a = Scatter(grad_down[..., :down_half], zx[::-1], zx, down_rank)
    grad_down_b = Scatter(grad_down[..., down_half:], zx_turned[::-1], zx, down_rank)

    def backward(cot_rows, silu_gate, slope):
        d_active = dot_second(cot_rows, weight_down)
        d_up = (d_active * silu_gate.astype(jnp.float32)).astype(jnp.bfloat16)
        d_gate = (d_active * slope.astype(jnp.float32)).astype(jnp.bfloat16)
        return d_gate, d_up

    def terms_of(parts):
        def rows(at):
            return sum(dot(left[at], right) for dot, left, right in parts)

        return rows(slice(0, row_total)), rows(slice(row_total, None)).astype(jnp.bfloat16)

    def one_core(kept, sent):
        return kept + swap(sent, CORE).astype(jnp.float32)

    d_gate_far, d_up_far = backward(cot_far, silu_far, slope_far)
    d_hidden_far = one_core(
        *terms_of([(dot_second, d_gate_far, weight_gate), (dot_second, d_up_far, weight_up)])
    ).astype(jnp.bfloat16)
    (
        d_hidden_far, d_gate_far, d_up_far, cot_near, active_far, active_near,
        grad_down_a.buffer, grad_down_b.buffer,
    ) = tie(
        d_hidden_far, d_gate_far, d_up_far, cot_near, active_far, active_near,
        grad_down_a.buffer, grad_down_b.buffer,
    )
    d_hidden_side = swap(d_hidden_far, SIDE)
    d_gate_near, d_up_near = backward(cot_near, silu_near, slope_near)
    d_hidden_kept, d_hidden_sent = terms_of(
        [(dot_second, d_gate_near, weight_gate), (dot_second, d_up_near, weight_up)]
    )
    gate_rows = (2, 2, own_rows, quarter)
    grad_gate = Scatter(
        split(dot_first(hidden_near, d_gate_near) + dot_first(hidden_far, d_gate_far), gate_rows),
        zx_turned[::-1],
        zx + group,
    )
    out_kept, out_sent = terms_of([(dot_plain, active_far, weight_down)])
    (
        d_hidden_kept, d_hidden_sent, d_hidden_side, out_kept, out_sent, d_up_near, d_up_far,
        active_near, grad_gate.buffer,
    ) = advance(
        [grad_down_a, grad_down_b],
        d_hidden_kept, d_hidden_sent, d_hidden_side, out_kept, out_sent, d_up_near, d_up_far,
        active_near, grad_gate.buffer,
    )

    out_side = swap(one_core(out_kept, out_sent).astype(jnp.bfloat16), SIDE)
    d_hidden_b = one_core(d_hidden_kept, d_hidden_sent) + d_hidden_side.astype(jnp.float32)
    d_norm_input, grad_gain_two = norm_back(d_hidden_b, normed_b, scale_b, gain_two)
    d_after = cot_full + d_norm_input
    d_branch = d_after.astype(jnp.bfloat16)
    d_gated = dot_second(d_branch, weight_out)
    d_c = (d_gated * convolved).astype(jnp.bfloat16)
    d_conv = (d_gated * c_part).reshape(seq_count, local_rows, feature_width)
    padded_grad = jnp.pad(d_conv, ((0, 0), (tap_count - 1, tap_count - 1), (0, 0)))
    span = local_rows + tap_count - 1
    d_extended = tap_values[0] * padded_grad[:, tap_count - 1 : tap_count - 1 + span]
    for offset in range(1, tap_count):
        start_at = tap_count - 1 - offset
        d_extended = d_extended + tap_values[offset] * padded_grad[:, start_at : start_at + span]
    edge_terms = d_extended[:, : tap_count - 1, :]
    grad_up = Scatter(
        split(dot_first(hidden_near, d_up_near) + dot_first(hidden_far, d_up_far), gate_rows),
        zx_turned[::-1],
        zx + group,
    )
    edge_terms, grad_up.buffer, out_side, d_branch, d_c, d_conv, active_near = advance(
        [grad_gate, grad_down_a, grad_down_b],
        edge_terms, grad_up.buffer, out_side, d_branch, d_c, d_conv, active_near,
    )

    incoming = shifted(edge_terms, "seq", -1)
    held_all = route_a + [CORE]
    shape_all = (2,) * len(held_all) + (own_rows, half_width)
    shape_one = (2,) * len(held_all) + (own_rows, feature_width)
    grad_out = Scatter(
        dot_first(gated, d_branch).astype(jnp.bfloat16).reshape(shape_one), [CORE, None], held_all
    )
    grad_c = Scatter(
        dot_first(hidden_low, d_c).astype(jnp.bfloat16).reshape(shape_one), [CORE, None], held_all
    )
    incoming_full = jnp.pad(incoming, ((0, 0), (local_rows - (tap_count - 1), 0), (0, 0)))
    d_mixed = (d_extended[:, tap_count - 1 :, :] + incoming_full).reshape(row_total, feature_width)
    d_bv = jnp.concatenate(
        [(d_mixed * v_part).astype(jnp.bfloat16), (d_mixed * b_part).astype(jnp.bfloat16)], axis=1
    )
    grad_a = Scatter(
        dot_first(hidden_low, d_bv).astype(jnp.bfloat16).reshape(shape_all),
        [CORE] + route_a[::-1],
        held_all,
    )
    d_bv, d_c, d_conv, grad_a.buffer, grad_out.buffer, grad_c.buffer = advance(
        [grad_up, grad_gate, grad_down_a, grad_down_b],
        d_bv, d_c, d_conv, grad_a.buffer, grad_out.buffer, grad_c.buffer,
    )
    finish(grad_down_a, grad_down_b)
    down_owned = jnp.concatenate([grad_down_a.buffer, grad_down_b.buffer], axis=-1)
    down_owned = quarter_owner_swap(down_owned.astype(jnp.bfloat16))
    d_hidden = dot_second(d_bv, weight_bv) + dot_second(d_c, weight_c)
    d_hidden, down_owned, grad_up.buffer, grad_gate.buffer = advance(
        [grad_a, grad_out, grad_c], d_hidden, down_owned, grad_up.buffer, grad_gate.buffer
    )
    grad_b = Scatter(
        jnp.concatenate([grad_out.buffer, grad_c.buffer], axis=-1), route_b[::-1], route_b
    )

    grad_taps = jnp.stack(
        [
            jnp.sum(d_conv * extended[:, offset : offset + local_rows], axis=(0, 1))
            for offset in range(tap_count)
        ],
        axis=0,
    )
    d_first_norm, grad_gain_one = norm_back(d_hidden, normed_a, scale_a, gain_one)
    grad_tokens = (d_after + d_first_norm).reshape(seq_count, local_rows, feature_width)
    small_terms = jnp.concatenate(
        [grad_gain_one[None, :], grad_gain_two[None, :], grad_taps], axis=0
    )

    small_terms, grad_tokens, active_near, out_side = advance(
        [grad_a, grad_b, grad_up, grad_gate], small_terms, grad_tokens, active_near, out_side
    )
    finish(grad_gate)

    def owned_quarters(cores):
        both = jnp.stack(ordered(core, *cores), axis=1)
        mine = lax.dynamic_index_in_dim(both, side, 0, keepdims=False)
        send = lax.dynamic_index_in_dim(both, 1 - side, 0, keepdims=False)
        other = swap(send.astype(jnp.bfloat16), SIDE).astype(jnp.float32)
        low, high = ordered(side, mine, other)
        return jnp.concatenate([low[0], high[0], low[1], high[1]], axis=-1)

    def summed(values, dims):
        for dim in dims:
            values = values + swap(values, dim)
        return values

    gate_core = regroup(grad_gate.buffer, 0, core, CORE)
    small_terms = summed(small_terms, [CORE] + near)
    out_own = one_core(*terms_of([(dot_plain, active_near, weight_down)]))
    results = after_mix + (out_own + out_side.astype(jnp.float32))
    block_out = results.astype(jnp.bfloat16).reshape(seq_count, local_rows, feature_width)
    small_terms, block_out, *gate_core = advance(
        [grad_a, grad_b, grad_up], small_terms, block_out, *gate_core
    )
    finish(grad_up)
    gate_owned = owned_quarters(gate_core)
    up_core = regroup(grad_up.buffer, 0, core, CORE)
    small_terms = summed(small_terms, [SIDE] + outer + far[:-1])
    small_terms, gate_owned, *up_core = advance([grad_a, grad_b], small_terms, gate_owned, *up_core)
    up_owned = owned_quarters(up_core)
    small_terms = summed(small_terms, far[-1:])
    finish(grad_a, grad_b)
    owned_a, owned_b = grad_a.buffer, grad_b.buffer
    place = lax.axis_index("fsdp") * lax.axis_size("seq") + lax.axis_index("seq")
    small_owned = lax.dynamic_slice_in_dim(small_terms, place * own_rows, own_rows, axis=1)
    return (
        block_out,
        grad_tokens,
        small_owned[0],
        jnp.concatenate(
            [owned_a[:, :feature_width], owned_b[:, feature_width:], owned_a[:, feature_width:]],
            axis=1,
        ),
        small_owned[2:],
        owned_b[:, :feature_width],
        small_owned[1],
        gate_owned,
        up_owned,
        down_owned.astype(jnp.float32),
    )


def solution(mesh):
    return jax.shard_map(
        body,
        mesh=mesh,
        in_specs=(
            P("fsdp", "seq", None),
            P(("fsdp", "seq")),
            P(("fsdp", "seq"), None),
            P(None, ("fsdp", "seq")),
            P(("fsdp", "seq"), None),
            P(("fsdp", "seq")),
            P(("fsdp", "seq"), None),
            P(("fsdp", "seq"), None),
            P(("fsdp", "seq"), None),
            P("fsdp", "seq", None),
        ),
        out_specs=(
            P("fsdp", "seq", None),
            P("fsdp", "seq", None),
            P(("fsdp", "seq")),
            P(("fsdp", "seq"), None),
            P(None, ("fsdp", "seq")),
            P(("fsdp", "seq"), None),
            P(("fsdp", "seq")),
            P(("fsdp", "seq"), None),
            P(("fsdp", "seq"), None),
            P(("fsdp", "seq"), None),
        ),
        check_vma=False,
    )
```

time: 518 us -> 438 us (0.85)
  waiting for transfers between devices: 238 us -> 205 us
  local copies, waits for them, and re-layouts: 44.4 us -> 25.2 us
  other arithmetic: 45.8 us -> 31.6 us
  matrix products: 94.8 us -> 88 us
  starting transfers between devices: 83 us -> 77 us
    ppermute x65 -> x75, waiting for transfers between devices: 237 us -> 204 us  [swap(): lax.ppermute(value, axis, [(i, i ^ 1 << bit) for i in range(lax.axis_size...]
    dot_general x8 -> x13, matrix products: 40.1 us -> 32.8 us  [dot_second(): lax.dot_general(left_segment, right_segment, (((1,), (1,)), ((), ())), pr...]
    concatenate x1 -> x6, local copies, waits for them, and re-layouts: 6.9 us -> 0.33 us  [the longest x4 0.18 us: merge(): jnp.concatenate(self.parts, axis=0)]
    unnamed x147 -> x149, local copies, waits for them, and re-layouts: 17 us -> 11.1 us
    squeeze x21 -> x23, local copies, waits for them, and re-layouts: 10.3 us -> 4.76 us  [sent(): return lax.dynamic_index_in_dim(self.buffer, 1 - bit, axis, keepdims=False)]
    dot_general x6 -> x9, matrix products: 22.9 us -> 24.8 us  [dot_first(): lax.dot_general(left_segment, right_segment, (((0,), (0,)), ((), ())), pr...]
    convert_element_type x16 -> x21, other arithmetic: 12 us -> 10.5 us  [the longest x17 8.09 us: take(): self.buffer = total.astype(jnp.bfloat16) if self.left else total]
    dot_general x7 -> x11, matrix products: 31.8 us -> 30.4 us  [dot_plain(): jnp.dot(left_segment, right_segment, preferred_element_type=jnp.float32)]
  transfers between devices with their start and end apart: 69 -> 79, of which waited for: 37 -> 36; matrix products, arithmetic and copies ran while one was open for 17% -> 19% of each run, Pallas kernels for 0% -> 0%
where the time goes in v3:
time: 438 us; the launch traced here: 429 us
  waiting for transfers between devices  205 us (47%)
  matrix products  88 us (20%)
  starting transfers between devices  77 us (18%)
  other arithmetic  31.6 us (7%)
  local copies, waits for them, and re-layouts  25.2 us (6%)
    ppermute x75, waiting for transfers between devices, swap(): lax.ppermute(value, axis, [(i, i ^ 1 << bit) for i in range(lax.axis_size...  204 us
    ppermute x75, starting transfers between devices, swap(): lax.ppermute(value, axis, [(i, i ^ 1 << bit) for i in range(lax.axis_size...  70.1 us
    dot_general x13, matrix products, dot_second(): lax.dot_general(left_segment, right_segment, (((1,), (1,)), ((), ())), pr...  32.8 us
    dot_general x11, matrix products, dot_plain(): jnp.dot(left_segment, right_segment, preferred_element_type=jnp.float32)  30.4 us
    dot_general x9, matrix products, dot_first(): lax.dot_general(left_segment, right_segment, (((0,), (0,)), ((), ())), pr...  24.8 us
    unnamed x149, local copies, waits for them, and re-layouts  11.1 us
  transfers between devices with their start and end apart: 79, of which 36 were waited for; matrix products, arithmetic and copies ran while one was open for 19% of the time, Pallas kernels for 0%

profile of v3, /device:TPU:0, one launch (start us, length us, event | category | flops | bytes accessed | tf_op | source)
XLA Modules:
  0.0 429.5 jit_solution(11562135733908934481)
XLA Ops:
  7.9 3.7 collective-permute-start
  13.2 15.0 %collective-permute-done = bf16[32,2048]{1,0:T(8,128)(2,1)} collective-permute-done((bf16[32,2048]{1,0:T(8,128)(2,1)S(1)}, bf16[32,2048]{1,0:T(8,128)(2,1)}, u32[]{:S(2)}, u32[]{:S(2)}) %collective-permute-start) | collective-permute-done | bytes 131104 | tf_op jit(solution)/shard_map/ppermute | solution.py:28
  35.5 9.4 %collective-permute-done.8 = bf16[256,1024]{1,0:T(8,128)(2,1)S(1)} collective-permute-done((bf16[256,1024]{1,0:T(8,128)(2,1)S(1)}, bf16[256,1024]{1,0:T(8,128)(2,1)S(1)}, u32[]{:S(2)}, u32[]{:S(2)}) %collective-permute-start.8) | collective-permute-done | bytes 524320 | tf_op jit(solution)/shard_map/ppermute | solution.py:28
  50.7 9.5 %collective-permute-done.14 = bf16[2,2,32,1152]{3,2,1,0:T(8,128)(2,1)S(1)} collective-permute-done((bf16[2,2,32,1152]{3,2,1,0:T(8,128)(2,1)S(1)}, bf16[2,2,32,1152]{3,2,1,0:T(8,128)(2,1)S(1)}, u32[]{:S(2)}, u32[]{:S(2)}) %collective-permute-start.14) | collective-permute-done | bytes 294944 | tf_op jit(solution)/shard_map/ppermute | solution.py:28
  67.8 21.1 %collective-permute-done.18 = bf16[2,2,2,32,1152]{4,3,2,1,0:T(8,128)(2,1)S(1)} collective-permute-done((bf16[2,2,2,32,1152]{4,3,2,1,0:T(8,128)(2,1)S(1)}, bf16[2,2,2,32,1152]{4,3,2,1,0:T(8,128)(2,1)S(1)}, u32[]{:S(2)}, u32[]{:S(2)}) %collective-permute-start.18) | collective-permute-done | bytes 589856 | tf_op jit(solution)/shard_map/ppermute | solution.py:28
  105.5 3.4 collective-permute-done.22
  115.6 3.6 fusion.27
  120.8 5.4 %collective-permute-done.25 = bf16[2,144,512]{2,1,0:T(8,128)(2,1)S(1)} collective-permute-done((bf16[2,144,512]{2,1,0:T(8,128)(2,1)S(1)}, bf16[2,144,512]{2,1,0:T(8,128)(2,1)S(1)}, u32[]{:S(2)}, u32[]{:S(2)}) %collective-permute-start.25) | collective-permute-done | bytes 294944 | tf_op jit(solution)/shard_map/ppermute | solution.py:28
  126.5 6.5 %collective-permute-done.26 = bf16[1,2,2,2,32,1152]{5,4,3,2,1,0:T(8,128)(2,1)S(1)} collective-permute-done((bf16[1,2,2,2,32,1152]{5,4,3,2,1,0:T(8,128)(2,1)S(1)}, bf16[1,2,2,2,32,1152]{5,4,3,2,1,0:T(8,128)(2,1)S(1)}, u32[]{:S(2)}, u32[]{:S(2)}) %collective-permute-start.26) | collective-permute-done | bytes 589856 | tf_op jit(solution)/shard_map/ppermute | solution.py:28
  138.2 11.3 %collective-permute-done.32 = bf16[1,2,2,2,32,1152]{5,4,3,2,1,0:T(8,128)(2,1)S(1)} collective-permute-done((bf16[1,2,2,2,32,1152]{5,4,3,2,1,0:T(8,128)(2,1)S(1)}, bf16[1,2,2,2,32,1152]{5,4,3,2,1,0:T(8,128)(2,1)S(1)}, u32[]{:S(2)}, u32[]{:S(2)}) %collective-permute-start.32) | collective-permute-done | bytes 589856 | tf_op jit(solution)/shard_map/ppermute | solution.py:28
  158.3 6.0 %multiply_convert_fusion.6 = (bf16[1024,1152]{1,0:T(8,128)(2,1)}, bf16[1024,1152]{1,0:T(8,128)(2,1)S(1)}, bf16[1024,1152]{1,0:T(8,128)(2,1)}) fusion(f32[1024,1152]{1,0:T(8,128)S(1)} %fusion.103, bf16[1024,1024]{1,0:T(8,128)(2,1)S(1)} %pad_maximum_fusion.7, bf16[1024,1152]{1,0:T(8,128)(2,1)S(1)} %bitcast.488), kind=kOutput, calls=%fused_computation.11 | convolution fusion | flops 2431254528 | bytes 16252928 | tf_op jit(solution)/shard_map/dot_general | solution.py:153
  175.0 5.2 %multiply_convert_fusion.4 = (bf16[1024,1152]{1,0:T(8,128)(2,1)S(1)}, bf16[1024,1152]{1,0:T(8,128)(2,1)S(1)}, bf16[1024,1152]{1,0:T(8,128)(2,1)}) fusion(f32[1024,1152]{1,0:T(8,128)S(1)} %fusion.105, bf16[1024,1024]{1,0:T(8,128)(2,1)S(1)} %constant_dynamic-update-slice_fusion.8, bf16[1024,1152]{1,0:T(8,128)(2,1)S(1)} %bitcast.489), kind=kOutput, calls=%fused_computation.6 | convolution fusion | flops 2431254528 | bytes 16252928 | tf_op jit(solution)/shard_map/dot_general | solution.py:153
  180.1 4.0 add_convert_fusion.2
  184.1 3.5 multiply_convert_fusion.3
  202.8 4.6 %multiply_convert_fusion.1 = (bf16[1024,1152]{1,0:T(8,128)(2,1)S(1)}, bf16[1024,1152]{1,0:T(8,128)(2,1)S(1)}) fusion(bf16[1024,1152]{1,0:T(8,128)(2,1)S(1)} %copy-done.69, bf16[1024,1152]{1,0:T(8,128)(2,1)} %get-tuple-element.367, bf16[1024,1024]{1,0:T(8,128)(2,1)S(1)} %copy-done.29, bf16[1152,512]{1,0:T(8,128)(2,1)S(1)} %bitcast.509, ...), kind=kOutput, calls=%fused_computation.3 | convolution fusion | flops 2427715584 | bytes 13893632 | tf_op jit(solution)/shard_map/dot_general | solution.py:163
  213.6 3.5 add_convert_fusion.1
  226.5 17.6 %collective-permute-done.40 = bf16[512,1024]{1,0:T(8,128)(2,1)S(1)} collective-permute-done((bf16[512,1024]{1,0:T(8,128)(2,1)S(1)}, bf16[512,1024]{1,0:T(8,128)(2,1)S(1)}, u32[]{:S(2)}, u32[]{:S(2)}) %collective-permute-start.40) | collective-permute-done | bytes 1048608 | tf_op jit(solution)/shard_map/ppermute | solution.py:28
  244.3 3.4 collective-permute-done.41
  256.3 3.7 add_convert_fusion
  267.9 16.8 %collective-permute-done.45 = bf16[512,1024]{1,0:T(8,128)(2,1)S(1)} collective-permute-done((bf16[512,1024]{1,0:T(8,128)(2,1)S(1)}, bf16[512,1024]{1,0:T(8,128)(2,1)S(1)}, u32[]{:S(2)}, u32[]{:S(2)}) %collective-permute-start.45) | collective-permute-done | bytes 1048608 | tf_op jit(solution)/shard_map/ppermute | solution.py:28
  300.2 10.3 %collective-permute-done.51 = bf16[2,2,2,32,1152]{4,3,2,1,0:T(8,128)(2,1)S(1)} collective-permute-done((bf16[2,2,2,32,1152]{4,3,2,1,0:T(8,128)(2,1)S(1)}, bf16[2,2,2,32,1152]{4,3,2,1,0:T(8,128)(2,1)S(1)}, u32[]{:S(2)}, u32[]{:S(2)}) %collective-permute-start.51) | collective-permute-done | bytes 589856 | tf_op jit(solution)/shard_map/ppermute | solution.py:28
  310.7 7.9 %collective-permute-done.50 = bf16[2,2,2,2,32,1152]{5,4,3,2,1,0:T(8,128)(2,1)S(1)} collective-permute-done((bf16[2,2,2,2,32,1152]{5,4,3,2,1,0:T(8,128)(2,1)S(1)}, bf16[2,2,2,2,32,1152]{5,4,3,2,1,0:T(8,128)(2,1)S(1)}, u32[]{:S(2)}, u32[]{:S(2)}) %collective-permute-start.50) | collective-permute-done | bytes 1179680 | tf_op jit(solution)/shard_map/ppermute | solution.py:28
  319.9 3.8 collective-permute-start.57
  328.2 4.1 fusion.100
  349.2 5.3 %collective-permute-done.61 = bf16[2,2,32,1152]{3,2,1,0:T(8,128)(2,1)} collective-permute-done((bf16[2,2,32,1152]{3,2,1,0:T(8,128)(2,1)}, bf16[2,2,32,1152]{3,2,1,0:T(8,128)(2,1)}, u32[]{:S(2)}, u32[]{:S(2)}) %collective-permute-start.61) | collective-permute-done | bytes 294944 | tf_op jit(solution)/shard_map/ppermute | solution.py:28
  355.6 5.2 %collective-permute-done.60 = bf16[2,2,2,32,1152]{4,3,2,1,0:T(8,128)(2,1)} collective-permute-done((bf16[2,2,2,32,1152]{4,3,2,1,0:T(8,128)(2,1)}, bf16[2,2,2,32,1152]{4,3,2,1,0:T(8,128)(2,1)}, u32[]{:S(2)}, u32[]{:S(2)}) %collective-permute-start.60) | collective-permute-done | bytes 589856 | tf_op jit(solution)/shard_map/ppermute | solution.py:28
  362.1 6.7 %collective-permute-done.59 = bf16[2,2,2,32,2048]{4,3,0,1,2:T(8,128)(2,1)} collective-permute-done((bf16[2,2,2,32,2048]{4,3,0,1,2:T(8,128)(2,1)}, bf16[2,2,2,32,2048]{4,3,0,1,2:T(8,128)(2,1)}, u32[]{:S(2)}, u32[]{:S(2)}) %collective-permute-start.59) | collective-permute-done | bytes 1048608 | tf_op jit(solution)/shard_map/ppermute | solution.py:28
  387.0 6.2 %collective-permute-done.67 = bf16[2,2,32,2048]{3,2,0,1:T(8,128)(2,1)S(1)} collective-permute-done((bf16[2,2,32,2048]{3,2,0,1:T(8,128)(2,1)S(1)}, bf16[2,2,32,2048]{3,2,0,1:T(8,128)(2,1)S(1)}, u32[]{:S(2)}, u32[]{:S(2)}) %collective-permute-start.67) | collective-permute-done | bytes 524320 | tf_op jit(solution)/shard_map/ppermute | solution.py:28
  393.4 3.2 collective-permute-done.66
  404.7 5.8 %collective-permute-done.70 = f32[5,1024]{1,0:T(8,128)S(1)} collective-permute-done((f32[5,1024]{1,0:T(8,128)S(1)}, f32[5,1024]{1,0:T(8,128)S(1)}, u32[]{:S(2)}, u32[]{:S(2)}) %collective-permute-start.70) | collective-permute-done | bytes 20512 | tf_op jit(solution)/shard_map/ppermute | solution.py:28
  411.6 5.8 %collective-permute-done.73 = bf16[2,32,2048]{2,1,0:T(8,128)(2,1)S(1)} collective-permute-done((bf16[2,32,2048]{2,1,0:T(8,128)(2,1)S(1)}, bf16[2,32,2048]{2,1,0:T(8,128)(2,1)S(1)}, u32[]{:S(2)}, u32[]{:S(2)}) %collective-permute-start.73) | collective-permute-done | bytes 262176 | tf_op jit(solution)/shard_map/ppermute | solution.py:28
  421.4 4.1 collective-permute-done.75
  (493 shorter events, 200.7 us)
Async XLA Ops:
  7.9 20.3 %collective-permute-start = (bf16[32,2048]{1,0:T(8,128)(2,1)S(1)}, bf16[32,2048]{1,0:T(8,128)(2,1)}, u32[]{:S(2)}, u32[]{:S(2)}) collective-permute-start(bf16[32,2048]{1,0:T(8,128)(2,1)S(1)} %pad_maximum_fusion.36), channel_id=1, source_target_pairs={{0,8},{2,10},{4,12},{6,14},{8,0},{10,2},{12,4},{14,6},{16,24},{18,... | collective-permute-start | bytes 393224 | tf_op jit(solution)/shard_map/ppermute | solution.py:28
  11.8 17.4 %collective-permute-start.4 = (bf16[32,2176]{1,0:T(8,128)(2,1)S(1)}, bf16[32,2176]{1,0:T(8,128)(2,1)}, u32[]{:S(2)}, u32[]{:S(2)}) collective-permute-start(bf16[32,2176]{1,0:T(8,128)(2,1)S(1)} %fusion.91), channel_id=1, source_target_pairs={{0,16},{2,18},{4,20},{6,22},{8,24},{10,26},{12,28},{14,30},{16,0},... | collective-permute-start | bytes 417800 | tf_op jit(solution)/shard_map/ppermute | solution.py:28
  47.9 15.2 %collective-permute-start.13 = (bf16[2,2,32,1152]{3,2,1,0:T(8,128)(2,1)S(1)}, bf16[2,2,32,1152]{3,2,1,0:T(8,128)(2,1)S(1)}, u32[]{:S(2)}, u32[]{:S(2)}) collective-permute-start(bf16[2,2,32,1152]{3,2,1,0:T(8,128)(2,1)S(1)} %pad_maximum_fusion.31), channel_id=1, source_target_pairs={{0,16},{2,18},{4,20},{6,22},{8,24},{10,26},{12,28},{14,30},{16,0},... | collective-permute-start | bytes 884744 | tf_op jit(solution)/shard_map/ppermute | solution.py:28
  63.7 25.1 %collective-permute-start.18 = (bf16[2,2,2,32,1152]{4,3,2,1,0:T(8,128)(2,1)S(1)}, bf16[2,2,2,32,1152]{4,3,2,1,0:T(8,128)(2,1)S(1)}, u32[]{:S(2)}, u32[]{:S(2)}) collective-permute-start(bf16[2,2,2,32,1152]{4,3,2,1,0:T(8,128)(2,1)S(1)} %pad_maximum_fusion.21), channel_id=1, source_target_pairs={{0,16},{2,18},{4,20},{6,22},{8,24},{10,26},{12,28},{14,30},{16,0},... | collective-permute-start | bytes 1769480 | tf_op jit(solution)/shard_map/ppermute | solution.py:28
  64.4 24.6 %collective-permute-start.17 = (bf16[2,2,2,32,1152]{4,3,2,1,0:T(8,128)(2,1)S(1)}, bf16[2,2,2,32,1152]{4,3,2,1,0:T(8,128)(2,1)S(1)}, u32[]{:S(2)}, u32[]{:S(2)}) collective-permute-start(bf16[2,2,2,32,1152]{4,3,2,1,0:T(8,128)(2,1)S(1)} %pad_maximum_fusion.20), channel_id=1, source_target_pairs={{0,8},{2,10},{4,12},{6,14},{8,0},{10,2},{12,4},{14,6},{16,24},{18,... | collective-permute-start | bytes 1769480 | tf_op jit(solution)/shard_map/ppermute | solution.py:28
  65.9 23.8 %collective-permute-start.16 = (bf16[2,2,2,32,2176]{4,3,2,1,0:T(8,128)(2,1)S(1)}, bf16[2,2,2,32,2176]{4,3,2,1,0:T(8,128)(2,1)S(1)}, u32[]{:S(2)}, u32[]{:S(2)}) collective-permute-start(bf16[2,2,2,32,2176]{4,3,2,1,0:T(8,128)(2,1)S(1)} %pad_maximum_fusion.15), channel_id=1, source_target_pairs={{0,4},{2,6},{4,0},{6,2},{8,12},{10,14},{12,8},{14,10},{16,20},{18,... | collective-permute-start | bytes 3342344 | tf_op jit(solution)/shard_map/ppermute | solution.py:28
  66.5 22.9 %collective-permute-start.15 = (bf16[2,2,2,32,2048]{4,3,2,1,0:T(8,128)(2,1)S(1)}, bf16[2,2,2,32,2048]{4,3,2,1,0:T(8,128)(2,1)S(1)}, u32[]{:S(2)}, u32[]{:S(2)}) collective-permute-start(bf16[2,2,2,32,2048]{4,3,2,1,0:T(8,128)(2,1)S(1)} %pad_maximum_fusion.16), channel_id=1, source_target_pairs={{0,1},{1,0},{2,3},{3,2},{4,5},{5,4},{6,7},{7,6},{8,9},{9,8},{10,11... | collective-permute-start | bytes 3145736 | tf_op jit(solution)/shard_map/ppermute | solution.py:28
  90.8 43.5 %collective-permute-start.29 = (bf16[512,1024]{1,0:T(8,128)(2,1)S(1)}, bf16[512,1024]{1,0:T(8,128)(2,1)S(1)}, u32[]{:S(2)}, u32[]{:S(2)}) collective-permute-start(bf16[512,1024]{1,0:T(8,128)(2,1)S(1)} %bitcast.474), channel_id=1, source_target_pairs={{0,2},{2,0},{4,6},{6,4},{8,10},{10,8},{12,14},{14,12},{16,18},{18,... | collective-permute-start | bytes 3145736 | tf_op jit(solution)/shard_map/ppermute | solution.py:28
  92.6 16.3 %collective-permute-start.22 = (bf16[1,2,2,2,32,1152]{5,4,3,2,1,0:T(8,128)(2,1)S(1)}, bf16[1,2,2,2,32,1152]{5,4,3,2,1,0:T(8,128)(2,1)S(1)}, u32[]{:S(2)}, u32[]{:S(2)}) collective-permute-start(bf16[1,2,2,2,32,1152]{5,4,3,2,1,0:T(8,128)(2,1)S(1)} %slice.255), channel_id=1, source_target_pairs={{0,4},{2,6},{4,0},{6,2},{8,12},{10,14},{12,8},{14,10},{16,20},{18,... | collective-permute-start | bytes 1769480 | tf_op jit(solution)/shard_map/ppermute | solution.py:28
  94.4 39.1 %collective-permute-start.27 = (bf16[1,2,2,2,32,1152]{5,4,3,2,1,0:T(8,128)(2,1)S(1)}, bf16[1,2,2,2,32,1152]{5,4,3,2,1,0:T(8,128)(2,1)S(1)}, u32[]{:S(2)}, u32[]{:S(2)}) collective-permute-start(bf16[1,2,2,2,32,1152]{5,4,3,2,1,0:T(8,128)(2,1)S(1)} %slice.268), channel_id=1, source_target_pairs={{0,4},{2,6},{4,0},{6,2},{8,12},{10,14},{12,8},{14,10},{16,20},{18,... | collective-permute-start | bytes 1769480 | tf_op jit(solution)/shard_map/ppermute | solution.py:28
  108.9 24.1 %collective-permute-start.26 = (bf16[1,2,2,2,32,1152]{5,4,3,2,1,0:T(8,128)(2,1)S(1)}, bf16[1,2,2,2,32,1152]{5,4,3,2,1,0:T(8,128)(2,1)S(1)}, u32[]{:S(2)}, u32[]{:S(2)}) collective-permute-start(bf16[1,2,2,2,32,1152]{5,4,3,2,1,0:T(8,128)(2,1)S(1)} %slice.267), channel_id=1, source_target_pairs={{0,4},{2,6},{4,0},{6,2},{8,12},{10,14},{12,8},{14,10},{16,20},{18,... | collective-permute-start | bytes 1769480 | tf_op jit(solution)/shard_map/ppermute | solution.py:28
  133.5 16.0 %collective-permute-start.28 = (bf16[512,1024]{1,0:T(8,128)(2,1)S(1)}, bf16[512,1024]{1,0:T(8,128)(2,1)S(1)}, u32[]{:S(2)}, u32[]{:S(2)}) collective-permute-start(bf16[512,1024]{1,0:T(8,128)(2,1)S(1)} %multiply_convert_fusion.10), channel_id=1, source_target_pairs={{0,2},{2,0},{4,6},{6,4},{8,10},{10,8},{12,14},{14,12},{16,18},{18,... | collective-permute-start | bytes 3145736 | tf_op jit(solution)/shard_map/ppermute | solution.py:28
  133.7 15.8 %collective-permute-start.32 = (bf16[1,2,2,2,32,1152]{5,4,3,2,1,0:T(8,128)(2,1)S(1)}, bf16[1,2,2,2,32,1152]{5,4,3,2,1,0:T(8,128)(2,1)S(1)}, u32[]{:S(2)}, u32[]{:S(2)}) collective-permute-start(bf16[1,2,2,2,32,1152]{5,4,3,2,1,0:T(8,128)(2,1)S(1)} %slice.270), channel_id=1, source_target_pairs={{0,4},{2,6},{4,0},{6,2},{8,12},{10,14},{12,8},{14,10},{16,20},{18,... | collective-permute-start | bytes 1769480 | tf_op jit(solution)/shard_map/ppermute | solution.py:28
  134.6 15.1 %collective-permute-start.31 = (bf16[256,1024]{1,0:T(8,128)(2,1)S(1)}, bf16[256,1024]{1,0:T(8,128)(2,1)S(1)}, u32[]{:S(2)}, u32[]{:S(2)}) collective-permute-start(bf16[256,1024]{1,0:T(8,128)(2,1)S(1)} %slice.269), channel_id=1, source_target_pairs={{0,1},{1,0},{2,3},{3,2},{4,5},{5,4},{6,7},{7,6},{8,9},{9,8},{10,11... | collective-permute-start | bytes 1572872 | tf_op jit(solution)/shard_map/ppermute | solution.py:28
  135.8 16.1 %collective-permute-start.33 = (bf16[1,2,144,512]{3,2,1,0:T(8,128)(2,1)S(1)}, bf16[1,2,144,512]{3,2,1,0:T(8,128)(2,1)S(1)}, u32[]{:S(2)}, u32[]{:S(2)}) collective-permute-start(bf16[1,2,144,512]{3,2,1,0:T(8,128)(2,1)S(1)} %slice.271), channel_id=1, source_target_pairs={{0,16},{2,18},{4,20},{6,22},{8,24},{10,26},{12,28},{14,30},{16,0},... | collective-permute-start | bytes 884744 | tf_op jit(solution)/shard_map/ppermute | solution.py:28
  151.9 15.2 %collective-permute-start.37 = (bf16[1,2,144,512]{3,2,0,1:T(8,128)(2,1)S(1)}, bf16[1,2,144,512]{3,2,0,1:T(8,128)(2,1)S(1)}, u32[]{:S(2)}, u32[]{:S(2)}) collective-permute-start(bf16[1,2,144,512]{3,2,0,1:T(8,128)(2,1)S(1)} %slice.275), channel_id=1, source_target_pairs={{0,8},{2,10},{4,12},{6,14},{8,0},{10,2},{12,4},{14,6},{16,24},{18,... | collective-permute-start | bytes 884744 | tf_op jit(solution)/shard_map/ppermute | solution.py:28
  152.8 16.0 %collective-permute-start.36 = (bf16[256,1024]{1,0:T(8,128)(2,1)S(1)}, bf16[256,1024]{1,0:T(8,128)(2,1)S(1)}, u32[]{:S(2)}, u32[]{:S(2)}) collective-permute-start(bf16[256,1024]{1,0:T(8,128)(2,1)S(1)} %slice.274), channel_id=1, source_target_pairs={{0,1},{1,0},{2,3},{3,2},{4,5},{5,4},{6,7},{7,6},{8,9},{9,8},{10,11... | collective-permute-start | bytes 1572872 | tf_op jit(solution)/shard_map/ppermute | solution.py:28
  153.8 14.9 %collective-permute-start.35 = (bf16[1,2,144,512]{3,2,1,0:T(8,128)(2,1)S(1)}, bf16[1,2,144,512]{3,2,1,0:T(8,128)(2,1)S(1)}, u32[]{:S(2)}, u32[]{:S(2)}) collective-permute-start(bf16[1,2,144,512]{3,2,1,0:T(8,128)(2,1)S(1)} %slice.273), channel_id=1, source_target_pairs={{0,16},{2,18},{4,20},{6,22},{8,24},{10,26},{12,28},{14,30},{16,0},... | collective-permute-start | bytes 884744 | tf_op jit(solution)/shard_map/ppermute | solution.py:28
  218.6 25.5 %collective-permute-start.40 = (bf16[512,1024]{1,0:T(8,128)(2,1)S(1)}, bf16[512,1024]{1,0:T(8,128)(2,1)S(1)}, u32[]{:S(2)}, u32[]{:S(2)}) collective-permute-start(bf16[512,1024]{1,0:T(8,128)(2,1)S(1)} %add_convert_fusion.6), channel_id=1, source_target_pairs={{0,1},{1,0},{2,3},{3,2},{4,5},{5,4},{6,7},{7,6},{8,9},{9,8},{10,11... | collective-permute-start | bytes 3145736 | tf_op jit(solution)/shard_map/ppermute | solution.py:28
  219.7 24.4 %collective-permute-start.42 = (bf16[2,2,144,512]{3,2,0,1:T(8,128)(2,1)S(1)}, bf16[2,2,144,512]{3,2,0,1:T(8,128)(2,1)S(1)}, u32[]{:S(2)}, u32[]{:S(2)}) collective-permute-start(bf16[2,2,144,512]{3,2,0,1:T(8,128)(2,1)S(1)} %dynamic-slice_bitcast_fusion.6), channel_id=1, source_target_pairs={{0,4},{2,6},{4,0},{6,2},{8,12},{10,14},{12,8},{14,10},{16,20},{18,... | collective-permute-start | bytes 1769480 | tf_op jit(solution)/shard_map/ppermute | solution.py:28
  221.3 26.4 %collective-permute-start.41 = (bf16[2,2,144,512]{3,2,1,0:T(8,128)(2,1)S(1)}, bf16[2,2,144,512]{3,2,1,0:T(8,128)(2,1)S(1)}, u32[]{:S(2)}, u32[]{:S(2)}) collective-permute-start(bf16[2,2,144,512]{3,2,1,0:T(8,128)(2,1)S(1)} %dynamic-slice_bitcast_fusion.7), channel_id=1, source_target_pairs={{0,4},{2,6},{4,0},{6,2},{8,12},{10,14},{12,8},{14,10},{16,20},{18,... | collective-permute-start | bytes 1769480 | tf_op jit(solution)/shard_map/ppermute | solution.py:28
  251.6 33.5 %collective-permute-start.48 = (bf16[2,144,512]{2,1,0:T(8,128)(2,1)S(1)}, bf16[2,144,512]{2,1,0:T(8,128)(2,1)S(1)}, u32[]{:S(2)}, u32[]{:S(2)}) collective-permute-start(bf16[2,144,512]{2,1,0:T(8,128)(2,1)S(1)} %dynamic-slice_bitcast_fusion.16), channel_id=1, source_target_pairs={{0,8},{2,10},{4,12},{6,14},{8,0},{10,2},{12,4},{14,6},{16,24},{18,... | collective-permute-start | bytes 884744 | tf_op jit(solution)/shard_map/ppermute | solution.py:28
  251.7 34.0 %collective-permute-start.47 = (bf16[2,144,512]{2,1,0:T(8,128)(2,1)S(1)}, bf16[2,144,512]{2,1,0:T(8,128)(2,1)S(1)}, u32[]{:S(2)}, u32[]{:S(2)}) collective-permute-start(bf16[2,144,512]{2,1,0:T(8,128)(2,1)S(1)} %dynamic-slice_bitcast_fusion.17), channel_id=1, source_target_pairs={{0,16},{2,18},{4,20},{6,22},{8,24},{10,26},{12,28},{14,30},{16,0},... | collective-permute-start | bytes 884744 | tf_op jit(solution)/shard_map/ppermute | solution.py:28
  254.8 30.0 %collective-permute-start.46 = (bf16[2,2,2,2,32,1152]{5,4,3,2,1,0:T(8,128)(2,1)S(1)}, bf16[2,2,2,2,32,1152]{5,4,3,2,1,0:T(8,128)(2,1)S(1)}, u32[]{:S(2)}, u32[]{:S(2)}) collective-permute-start(bf16[2,2,2,2,32,1152]{5,4,3,2,1,0:T(8,128)(2,1)S(1)} %dynamic-slice_bitcast_fusion.1), channel_id=1, source_target_pairs={{0,4},{2,6},{4,0},{6,2},{8,12},{10,14},{12,8},{14,10},{16,20},{18,... | collective-permute-start | bytes 3538952 | tf_op jit(solution)/shard_map/ppermute | solution.py:28
  260.4 24.3 %collective-permute-start.45 = (bf16[512,1024]{1,0:T(8,128)(2,1)S(1)}, bf16[512,1024]{1,0:T(8,128)(2,1)S(1)}, u32[]{:S(2)}, u32[]{:S(2)}) collective-permute-start(bf16[512,1024]{1,0:T(8,128)(2,1)S(1)} %add_convert_fusion.4), channel_id=1, source_target_pairs={{0,1},{1,0},{2,3},{3,2},{4,5},{5,4},{6,7},{7,6},{8,9},{9,8},{10,11... | collective-permute-start | bytes 3145736 | tf_op jit(solution)/shard_map/ppermute | solution.py:28
  292.5 18.1 %collective-permute-start.51 = (bf16[2,2,2,32,1152]{4,3,2,1,0:T(8,128)(2,1)S(1)}, bf16[2,2,2,32,1152]{4,3,2,1,0:T(8,128)(2,1)S(1)}, u32[]{:S(2)}, u32[]{:S(2)}) collective-permute-start(bf16[2,2,2,32,1152]{4,3,2,1,0:T(8,128)(2,1)S(1)} %dynamic-slice_bitcast_fusion.5), channel_id=1, source_target_pairs={{0,8},{2,10},{4,12},{6,14},{8,0},{10,2},{12,4},{14,6},{16,24},{18,... | collective-permute-start | bytes 1769480 | tf_op jit(solution)/shard_map/ppermute | solution.py:28
  293.0 25.6 %collective-permute-start.50 = (bf16[2,2,2,2,32,1152]{5,4,3,2,1,0:T(8,128)(2,1)S(1)}, bf16[2,2,2,2,32,1152]{5,4,3,2,1,0:T(8,128)(2,1)S(1)}, u32[]{:S(2)}, u32[]{:S(2)}) collective-permute-start(bf16[2,2,2,2,32,1152]{5,4,3,2,1,0:T(8,128)(2,1)S(1)} %dynamic-slice_bitcast_fusion), channel_id=1, source_target_pairs={{0,4},{2,6},{4,0},{6,2},{8,12},{10,14},{12,8},{14,10},{16,20},{18,... | collective-permute-start | bytes 3538952 | tf_op jit(solution)/shard_map/ppermute | solution.py:28
  337.9 16.6 %collective-permute-start.61 = (bf16[2,2,32,1152]{3,2,1,0:T(8,128)(2,1)}, bf16[2,2,32,1152]{3,2,1,0:T(8,128)(2,1)}, u32[]{:S(2)}, u32[]{:S(2)}) collective-permute-start(bf16[2,2,32,1152]{3,2,1,0:T(8,128)(2,1)} %dynamic-slice_bitcast_fusion.15), channel_id=1, source_target_pairs={{0,16},{2,18},{4,20},{6,22},{8,24},{10,26},{12,28},{14,30},{16,0},... | collective-permute-start | bytes 884744 | tf_op jit(solution)/shard_map/ppermute | solution.py:28
  338.8 21.9 %collective-permute-start.60 = (bf16[2,2,2,32,1152]{4,3,2,1,0:T(8,128)(2,1)}, bf16[2,2,2,32,1152]{4,3,2,1,0:T(8,128)(2,1)}, u32[]{:S(2)}, u32[]{:S(2)}) collective-permute-start(bf16[2,2,2,32,1152]{4,3,2,1,0:T(8,128)(2,1)} %dynamic-slice_bitcast_fusion.4), channel_id=1, source_target_pairs={{0,8},{2,10},{4,12},{6,14},{8,0},{10,2},{12,4},{14,6},{16,24},{18,... | collective-permute-start | bytes 1769480 | tf_op jit(solution)/shard_map/ppermute | solution.py:28
  343.7 25.1 %collective-permute-start.59 = (bf16[2,2,2,32,2048]{4,3,0,1,2:T(8,128)(2,1)}, bf16[2,2,2,32,2048]{4,3,0,1,2:T(8,128)(2,1)}, u32[]{:S(2)}, u32[]{:S(2)}) collective-permute-start(bf16[2,2,2,32,2048]{4,3,0,1,2:T(8,128)(2,1)} %dynamic-slice_bitcast_fusion.2), channel_id=1, source_target_pairs={{0,4},{2,6},{4,0},{6,2},{8,12},{10,14},{12,8},{14,10},{16,20},{18,... | collective-permute-start | bytes 3145736 | tf_op jit(solution)/shard_map/ppermute | solution.py:28
  347.3 24.8 %collective-permute-start.58 = (bf16[2,2,2,32,2048]{4,3,1,0,2:T(8,128)(2,1)}, bf16[2,2,2,32,2048]{4,3,1,0,2:T(8,128)(2,1)S(1)}, u32[]{:S(2)}, u32[]{:S(2)}) collective-permute-start(bf16[2,2,2,32,2048]{4,3,1,0,2:T(8,128)(2,1)} %dynamic-slice_bitcast_fusion.3), channel_id=1, source_target_pairs={{0,1},{1,0},{2,3},{3,2},{4,5},{5,4},{6,7},{7,6},{8,9},{9,8},{10,11... | collective-permute-start | bytes 3145736 | tf_op jit(solution)/shard_map/ppermute | solution.py:28
  374.9 18.5 %collective-permute-start.68 = (bf16[2,2,32,1152]{3,2,1,0:T(8,128)(2,1)S(1)}, bf16[2,2,32,1152]{3,2,1,0:T(8,128)(2,1)S(1)}, u32[]{:S(2)}, u32[]{:S(2)}) collective-permute-start(bf16[2,2,32,1152]{3,2,1,0:T(8,128)(2,1)S(1)} %dynamic-slice_bitcast_fusion.12), channel_id=1, source_target_pairs={{0,16},{2,18},{4,20},{6,22},{8,24},{10,26},{12,28},{14,30},{16,0},... | collective-permute-start | bytes 884744 | tf_op jit(solution)/shard_map/ppermute | solution.py:28
  (118 other events, 1020.7 us)
